TPU v7x, 256 devices: a whole 4x4x8 slice. The times are simulated.
256 devices in a mesh: dp: 32 (over z, x), seq: 8 (over y, core).
Axes of the slice: x: 4, y: 4, z: 8, core: 2. Of those that a mesh axis runs over, the one named last changes fastest.
Arguments:
- query: bfloat16 [32768, 2048], P(('dp', 'seq')), may hold values from -6 to 6
- key_rows: bfloat16 [32768, 1024], P(('dp', 'seq')), may hold values from -6 to 6
- value_rows: bfloat16 [32768, 1024], P(('dp', 'seq')), may hold values from -6 to 6
- attn_out: bfloat16 [32768, 2048], P(('dp', 'seq')), may hold values from -6 to 6
- out_grad: bfloat16 [32768, 2048], P(('dp', 'seq')), may hold values from -6 to 6
- source_row: int32 [32768], P(('dp', 'seq')), may hold values from 0 to 32767, as said below
- segment_ids: int32 [32768], P('dp'), may hold values from 0 to 7, as said below
Outputs:
- grad_query: bfloat16 [32768, 2048], P(('dp', 'seq'))
- grad_key: bfloat16 [32768, 1024], P(('dp', 'seq'))
- grad_value: bfloat16 [32768, 1024], P(('dp', 'seq'))
Inputs may be any that keep to these rules, and one draw needn't show every extreme that they name: source_row is a permutation of all rows; a row keeps its seq index; one rollout device sends at most 8 rows to one owner, and every owner takes exactly 8 rows from some rollout device; within one seq index, how many rows go from one device to another depends only on the difference of their dp indices. `segment_ids`: within each pack of 1024 rows the ids start at 0, never fall and rise by at most 1 from one row to the next; every pack holds exactly 8 pairs.
All inputs are finite; a program needn't handle non-finite values.
Results may differ from a plain program's by a relative error of at most 0.0049.
Values may be sent and summed in bfloat16 or wider, within the bound.
No kernel may reach another device: no remote copies, remote signals or barrier semaphores. Data moves between devices by JAX's collectives and lax.ppermute only.
A program may use at most 64 MiB of HBM per device.

v0:
```python
import functools

import jax
import jax.numpy as jnp
from jax import lax
from jax.experimental import pallas as pl
from jax.experimental.pallas import tpu as pltpu
from jax.sharding import PartitionSpec as P

HEAD_DIM = 128
N_DP = 32
N_SEQ = 8
ROWS = 128
GROUP = N_SEQ * ROWS
WIDTH = 6 * HEAD_DIM
LANES = 128
BLOCK = 256
CAPACITY = 56
EXTRA = 16

scaling = 1.0 / 12.0
softcap = 50.0

PARAMS = pltpu.CompilerParams(vmem_limit_bytes=28 * 1024 * 1024)
FULL = pltpu.CompilerParams(vmem_limit_bytes=60 * 1024 * 1024)


def iota(shape, dim):
    return lax.broadcasted_iota(jnp.int32, shape, dim)


def nt_dot(left, right):
    return lax.dot_general(left, right, (((1,), (1,)), ((), ())), preferred_element_type=jnp.float32)


def nn_dot(left, right):
    return jnp.dot(left, right, preferred_element_type=jnp.float32)


def pack_kernel(me_ref, query_hbm, key_hbm, value_hbm, out_hbm, grad_hbm, *refs):
    packed_refs = refs[:N_SEQ]
    query_ref, key_ref, value_ref, out_ref, grad_ref, delta_ref, sems = refs[N_SEQ:]
    pairs = (
        (grad_hbm, grad_ref),
        (out_hbm, out_ref),
        (query_hbm, query_ref),
        (key_hbm, key_ref),
        (value_hbm, value_ref),
    )
    copies = [
        pltpu.make_async_copy(source, target, sems.at[i])
        for i, (source, target) in enumerate(pairs)
    ]
    for copy in copies:
        copy.start()
    copies[0].wait()
    copies[1].wait()
    lane = iota((ROWS, LANES), 1)
    table = jnp.zeros((ROWS, LANES), jnp.float32)
    for head in range(2 * N_SEQ):
        cols = slice(head * HEAD_DIM, (head + 1) * HEAD_DIM)
        product = grad_ref[:, cols].astype(jnp.float32) * out_ref[:, cols].astype(jnp.float32)
        table = jnp.where(lane == head, jnp.sum(product, axis=1, keepdims=True), table)
    delta = table.T
    high = delta.astype(jnp.bfloat16).astype(jnp.float32)
    low = delta - high
    for group in range(N_SEQ):
        pair = slice(2 * group, 2 * group + 2)
        delta_ref[group] = jnp.concatenate(
            [high[pair], low[pair], jnp.zeros((4, LANES), jnp.float32)], axis=0
        )
    pad_cols = jnp.zeros((8, WIDTH - LANES), jnp.float32)
    for copy in copies[2:]:
        copy.wait()
    me = me_ref[0]
    for m in range(N_SEQ):
        group = jnp.bitwise_xor(me, m)
        two = pl.ds(pl.multiple_of(group * 256, 256), 256)
        one = pl.ds(pl.multiple_of(group * 128, 128), 128)
        rows = jnp.concatenate(
            [query_ref[:, two], key_ref[:, one], value_ref[:, one], grad_ref[:, two]], axis=1
        )
        extra = jnp.concatenate([delta_ref[group], pad_cols], axis=1)
        packed_refs[m][...] = jnp.concatenate([rows.astype(jnp.float32), extra], axis=0).astype(
            jnp.bfloat16
        )


def wide(rows):
    return jnp.concatenate([rows[s : s + 1] for s in range(N_SEQ)], axis=1)


def index_kernel(list_ref, segment_ref, rows_ref, cols_ref, request_ref, most_ref):
    listed = list_ref[...]
    source = (listed // GROUP).astype(jnp.float32)
    local_row = (listed % ROWS).astype(jnp.float32)
    segment = segment_ref[...].astype(jnp.float32)
    blank = jnp.zeros((LANES - 8, LANES), jnp.float32)
    source_cols = jnp.concatenate([source, blank], axis=0).T
    before = iota((ROWS, ROWS), 0) < iota((ROWS, ROWS), 1)
    slots = []
    for s in range(N_SEQ):
        mine = source[s : s + 1]
        hits = ((source_cols[:, s : s + 1] == mine) & before).astype(jnp.float32)
        for earlier in range(s):
            hits = hits + (source_cols[:, earlier : earlier + 1] == mine).astype(jnp.float32)
        slots.append(jnp.sum(hits, axis=0, keepdims=True))
    slot = jnp.concatenate(slots, axis=0)
    blank = jnp.zeros((LANES - 24, LANES), jnp.float32)
    turned = jnp.concatenate([source, slot, segment, blank], axis=0).T
    lane = iota((ROWS, LANES), 1)
    picks = []
    for s in range(N_SEQ):
        columns = jnp.where(lane == 0, turned[:, s : s + 1], 0.0)
        columns = jnp.where(lane == 1, turned[:, 8 + s : 9 + s], columns)
        columns = jnp.where(lane == 2, turned[:, 16 + s : 17 + s], columns)
        cols_ref[s * ROWS : (s + 1) * ROWS, :] = columns
        picks.append((lane.astype(jnp.float32) == turned[:, 8 + s : 9 + s] + 1.0).astype(jnp.float32))
    rows_ref[0:8, :] = source
    rows_ref[8:16, :] = slot
    rows_ref[16:24, :] = segment
    pick = jnp.concatenate(picks, axis=0).astype(jnp.bfloat16)
    from_source = iota((N_DP, GROUP), 0).astype(jnp.float32) == wide(source)
    column = (iota((1, GROUP), 1) // ROWS).astype(jnp.float32)
    low = jnp.where(from_source, wide(local_row) + 1.0, 0.0).astype(jnp.bfloat16)
    high = jnp.where(from_source, column, 0.0).astype(jnp.bfloat16)
    table = nn_dot(low, pick) + float(ROWS) * nn_dot(high, pick)
    request_ref[...] = table.astype(jnp.int32)
    most_ref[0, 0] = (jnp.max(slot) + 1.0).astype(jnp.int32)


def request_picks(turned, group, first, capacity, width):
    column = jnp.concatenate(
        [turned[first : first + capacity, d : d + 1] for d in range(8 * group, 8 * group + 8)], axis=0
    )
    row_id = iota((8 * capacity, width), 1).astype(jnp.float32)
    return (column == row_id).astype(jnp.float32).astype(jnp.bfloat16)


def turned_requests(request_ref):
    blank = jnp.zeros((LANES - N_DP, LANES), jnp.float32)
    turned = jnp.concatenate([request_ref[...].astype(jnp.float32), blank], axis=0).T
    delta_id = (iota((LANES, LANES), 1) + GROUP).astype(jnp.float32)
    return jnp.where(iota((LANES, LANES), 0) == 0, delta_id, turned - 1.0)


def join_columns(me_ref, parts, ext_ref, delta_ref):
    for m in range(N_SEQ):
        column = jnp.bitwise_xor(me_ref[0], m)
        ext_ref[pl.ds(pl.multiple_of(column * ROWS, ROWS), ROWS), :] = parts[m][:ROWS, :]
        if delta_ref is not None:
            delta_ref[column] = parts[m][ROWS:, :LANES].astype(jnp.float32)


def send_extra_kernel(me_ref, request_ref, *refs):
    parts, (sent_ref, ext_ref) = refs[:N_SEQ], refs[N_SEQ:]
    group_rows = 8 * EXTRA
    turned = turned_requests(request_ref)
    join_columns(me_ref, parts, ext_ref, None)
    for group in range(N_DP // 8):
        pick = request_picks(turned, group, CAPACITY, EXTRA, GROUP)
        rows = slice(group * group_rows, (group + 1) * group_rows)
        sent_ref[rows, :] = nn_dot(pick, ext_ref[...]).astype(jnp.bfloat16)


def send_kernel(me_ref, most_ref, request_ref, *refs):
    parts, (sent_ref, pick_ref, ext_ref, place_ref, delta_ref) = refs[:N_SEQ], refs[N_SEQ:]
    capacity = CAPACITY
    group_rows = 8 * capacity
    turned = turned_requests(request_ref)
    join_columns(me_ref, parts, ext_ref, delta_ref)
    delta = jnp.concatenate([delta_ref[s] for s in range(N_SEQ)], axis=1)

    def places(pick, group, first, count):
        index = iota((8, 8 * count), 1)
        owner = index // count
        value = jnp.where(
            iota((8, 8 * count), 0) == 0, owner + 8 * group, index - owner * count + first
        )
        return nn_dot(value.astype(jnp.float32).astype(jnp.bfloat16), pick[:, :GROUP])

    place = jnp.zeros((8, GROUP), jnp.float32)
    for group in range(N_DP // 8):
        pick = request_picks(turned, group, 0, capacity, GROUP + LANES)
        pick_ref[group * group_rows : (group + 1) * group_rows, :] = pick
        place = place + places(pick, group, 0, capacity)
    place_ref[...] = place

    @pl.when(most_ref[0, 0] >= CAPACITY)
    def _():
        more = jnp.zeros((8, GROUP), jnp.float32)
        for group in range(N_DP // 8):
            pick = request_picks(turned, group, CAPACITY, EXTRA, GROUP)
            more = more + places(pick, group, CAPACITY, EXTRA)
        place_ref[...] += more

    place = place_ref[...]
    owner_of = place[0:1]
    slot_cols = []
    for s in range(N_SEQ):
        part = place[:, s * ROWS : (s + 1) * ROWS]
        blank = jnp.zeros((LANES - 8, LANES), jnp.float32)
        slot_cols.append(jnp.concatenate([part, blank], axis=0).T[:, 1:2])
    slot_col = jnp.concatenate(slot_cols, axis=0)
    lane = iota((GROUP, LANES), 1).astype(jnp.float32)
    to_owner = iota((N_DP, GROUP), 0).astype(jnp.float32) == owner_of
    tail = jnp.zeros((2 * N_DP, LANES), jnp.float32)
    for head in range(2):
        spread = jnp.concatenate(
            [jnp.where(to_owner, delta[c : c + 1], 0.0) for c in (head, 2 + head)], axis=0
        )
        slot_pick = (slot_col + (64.0 * head - 1.0) == lane).astype(jnp.float32)
        tail = tail + nn_dot(spread.astype(jnp.bfloat16), slot_pick.astype(jnp.bfloat16))
    tail = jnp.concatenate(
        [tail[:N_DP], tail[N_DP:], jnp.zeros((N_DP, WIDTH - 2 * LANES), jnp.float32)], axis=1
    )
    tail = jnp.concatenate([tail, jnp.zeros((LANES - N_DP, WIDTH), jnp.float32)], axis=0)
    ext_ref[GROUP:, :] = tail.astype(jnp.bfloat16)
    for group in range(N_DP // 8):
        rows = slice(group * group_rows, (group + 1) * group_rows)
        sent_ref[rows, :] = nn_dot(pick_ref[rows, :], ext_ref[...]).astype(jnp.bfloat16)


def attend_kernel(
    segment_ref, most_ref, arrived_ref, extra_ref, rows_ref, cols_ref, out_ref,
    x_ref, kt_ref, delta_ref, weight_ref, squash_ref, total_ref, gqt_ref, gk_ref, gv_ref,
):
    slots = N_DP * CAPACITY
    blocks = GROUP // BLOCK
    slot_id = iota((BLOCK, slots), 1).astype(jnp.float32)
    for block in range(blocks):
        rows = slice(block * BLOCK, (block + 1) * BLOCK)
        slot = cols_ref[rows, 1:2] + 1.0
        place = jnp.where(slot < CAPACITY, cols_ref[rows, 0:1] * float(CAPACITY) + slot, -1.0)
        pick = (place == slot_id).astype(jnp.float32).astype(jnp.bfloat16)
        x_ref[rows, :] = nn_dot(pick, arrived_ref[...]).astype(jnp.bfloat16)

    @pl.when(most_ref[0, 0] >= CAPACITY)
    def _():
        extra_id = iota((BLOCK, N_DP * EXTRA), 1).astype(jnp.float32)
        for block in range(blocks):
            rows = slice(block * BLOCK, (block + 1) * BLOCK)
            slot = cols_ref[rows, 1:2] - float(CAPACITY - 1)
            place = jnp.where(slot >= 0.0, cols_ref[rows, 0:1] * float(EXTRA) + slot, -1.0)
            pick = (place == extra_id).astype(jnp.float32).astype(jnp.bfloat16)
            x_ref[rows, :] += nn_dot(pick, extra_ref[...]).astype(jnp.bfloat16)

    for block in range(blocks):
        rows = slice(block * BLOCK, (block + 1) * BLOCK)
        kt_ref[:, rows] = x_ref[rows, 256:384].astype(jnp.float32).T.astype(jnp.bfloat16)
    first = iota((LANES, slots), 0) * CAPACITY == iota((LANES, slots), 1)
    first = first.astype(jnp.float32).astype(jnp.bfloat16)
    parts = nn_dot(first, arrived_ref[:, : 2 * LANES])
    source = wide(rows_ref[0:8, :])
    slot = wide(rows_ref[8:16, :])
    segment = wide(rows_ref[16:24, :])
    from_source = iota((LANES, GROUP), 0).astype(jnp.float32) == source
    from_source = from_source.astype(jnp.float32).astype(jnp.bfloat16)
    high = parts[:, :LANES].T.astype(jnp.bfloat16)
    low = parts[:, LANES:].T.astype(jnp.bfloat16)
    both = nn_dot(high, from_source) + nn_dot(low, from_source)
    place = iota((LANES, GROUP), 0).astype(jnp.float32)
    for head in range(2):
        delta_ref[head : head + 1, :] = jnp.sum(
            jnp.where(place == slot + 64.0 * head, both, 0.0), axis=0, keepdims=True
        )
    gk_ref[...] = jnp.zeros_like(gk_ref)
    gv_ref[...] = jnp.zeros_like(gv_ref)
    causal = iota((BLOCK, BLOCK), 0) <= iota((BLOCK, BLOCK), 1)
    causal = jnp.concatenate([causal.astype(jnp.float32)] * 2, axis=1) > 0.0
    for block in range(blocks):
        rows = slice(block * BLOCK, (block + 1) * BLOCK)
        queries = jnp.concatenate([x_ref[rows, 0:128], x_ref[rows, 128:256]], axis=0)
        grads = jnp.concatenate([x_ref[rows, 512:640], x_ref[rows, 640:768]], axis=0)
        delta = jnp.concatenate([delta_ref[0:1, rows], delta_ref[1:2, rows]], axis=1)
        segment_q = jnp.concatenate([segment[:, rows]] * 2, axis=1)

        def weigh(key_block):
            keys = slice(key_block * BLOCK, (key_block + 1) * BLOCK)
            score = nt_dot(x_ref[keys, 256:384], queries)
            squashed = jnp.tanh(score * (scaling / softcap))
            allowed = cols_ref[keys, 2:3] == segment_q
            if key_block == block:
                allowed = allowed & causal
            weights = jnp.where(allowed, jnp.exp(softcap * squashed), 0.0)
            weight_ref[keys, :] = weights
            squash_ref[keys, :] = squashed
            total = jnp.sum(weights, axis=0, keepdims=True)
            if key_block == block:
                total_ref[0:1, :] = total
            else:
                total_ref[0:1, :] += total

        def back(key_block):
            keys = slice(key_block * BLOCK, (key_block + 1) * BLOCK)
            probabilities = weight_ref[keys, :] * (1.0 / total_ref[0:1, :])
            gv_ref[keys, :] += nn_dot(probabilities.astype(jnp.bfloat16), grads)
            prob_grad = nt_dot(x_ref[keys, 384:512], grads)
            squashed = squash_ref[keys, :]
            score_grad = probabilities * (prob_grad - delta) * (1.0 - squashed * squashed)
            score_grad = score_grad.astype(jnp.bfloat16)
            gk_ref[keys, :] += nn_dot(score_grad, queries)
            part = nn_dot(kt_ref[:, keys], score_grad)
            if key_block == block:
                gqt_ref[...] = part
            else:
                gqt_ref[...] += part

        first_segment = segment_ref[block * BLOCK]
        for step in (weigh, back):
            step(block)
            for key_block in range(block):
                meets = segment_ref[(key_block + 1) * BLOCK - 1] == first_segment
                pl.when(meets)(functools.partial(step, key_block))
        turned = (gqt_ref[...].T * scaling).astype(jnp.bfloat16)
        out_ref[rows, 0:128] = turned[:BLOCK]
        out_ref[rows, 128:256] = turned[BLOCK:]
    out_ref[:, 256:384] = (gk_ref[...] * scaling).astype(jnp.bfloat16)
    out_ref[:, 384:512] = gv_ref[...].astype(jnp.bfloat16)


def unpack_kernel(returned_ref, query_ref, key_ref, value_ref):
    for group in range(N_SEQ):
        two = slice(2 * group * HEAD_DIM, 2 * (group + 1) * HEAD_DIM)
        one = slice(group * HEAD_DIM, (group + 1) * HEAD_DIM)
        query_ref[:, two] = returned_ref[group, :, 0:256]
        key_ref[:, one] = returned_ref[group, :, 256:384]
        value_ref[:, one] = returned_ref[group, :, 384:512]


def shape(dims, dtype=jnp.bfloat16):
    return jax.ShapeDtypeStruct(dims, dtype)


VMEM = pl.BlockSpec(memory_space=pltpu.VMEM)
SMEM = pl.BlockSpec(memory_space=pltpu.SMEM)


def cost(flops, moved, transcendentals=0):
    return pl.CostEstimate(flops=flops, bytes_accessed=moved, transcendentals=transcendentals)


def pack(me, query, key_rows, value_rows, attn_out, out_grad):
    return pl.pallas_call(
        pack_kernel,
        out_shape=[shape((ROWS + 8, WIDTH))] * N_SEQ,
        in_specs=[SMEM] + [pl.BlockSpec(memory_space=pltpu.HBM)] * 5,
        out_specs=[VMEM] * N_SEQ,
        scratch_shapes=[
            pltpu.VMEM((ROWS, 2048), jnp.bfloat16),
            pltpu.VMEM((ROWS, 1024), jnp.bfloat16),
            pltpu.VMEM((ROWS, 1024), jnp.bfloat16),
            pltpu.VMEM((ROWS, 2048), jnp.bfloat16),
            pltpu.VMEM((ROWS, 2048), jnp.bfloat16),
            pltpu.VMEM((N_SEQ, 8, LANES), jnp.float32),
            pltpu.SemaphoreType.DMA((5,)),
        ],
        compiler_params=FULL,
        name="pack",
    )(me, query, key_rows, value_rows, attn_out, out_grad)


def index(pack_list, segments):
    vmem = pl.BlockSpec(memory_space=pltpu.VMEM)
    return pl.pallas_call(
        index_kernel,
        out_shape=(
            shape((24, LANES), jnp.float32),
            shape((GROUP, LANES), jnp.float32),
            shape((N_DP, LANES), jnp.int32),
            shape((1, 1), jnp.int32),
        ),
        out_specs=(vmem, vmem, vmem, pl.BlockSpec(memory_space=pltpu.SMEM)),
        compiler_params=PARAMS,
        name="index",
    )(pack_list, segments.reshape(N_SEQ, ROWS))


def send(me, most, request, parts):
    return pl.pallas_call(
        send_kernel,
        out_shape=shape((N_DP * CAPACITY, WIDTH)),
        in_specs=[SMEM, SMEM] + [VMEM] * 9,
        scratch_shapes=[
            pltpu.VMEM((N_DP * CAPACITY, GROUP + LANES), jnp.bfloat16),
            pltpu.VMEM((GROUP + LANES, WIDTH), jnp.bfloat16),
            pltpu.VMEM((8, GROUP), jnp.float32),
            pltpu.VMEM((N_SEQ, 8, LANES), jnp.float32),
        ],
        compiler_params=PARAMS,
        cost_estimate=cost(2 * N_DP * CAPACITY * GROUP * WIDTH, 4_000_000),
        name="send",
    )(me, most, request, *parts)


def send_extra(me, request, parts):
    return pl.pallas_call(
        send_extra_kernel,
        out_shape=shape((N_DP * EXTRA, WIDTH)),
        in_specs=[SMEM] + [VMEM] * 9,
        scratch_shapes=[pltpu.VMEM((GROUP, WIDTH), jnp.bfloat16)],
        compiler_params=PARAMS,
        name="send_extra",
    )(me, request, *parts)


def attend(segments, most, arrived, extra, rows, cols):
    return pl.pallas_call(
        attend_kernel,
        out_shape=shape((GROUP, 4 * HEAD_DIM)),
        in_specs=[SMEM, SMEM, VMEM, VMEM, VMEM, VMEM],
        scratch_shapes=[
            pltpu.VMEM((GROUP, WIDTH), jnp.bfloat16),
            pltpu.VMEM((HEAD_DIM, GROUP), jnp.bfloat16),
            pltpu.VMEM((8, GROUP), jnp.float32),
            pltpu.VMEM((GROUP, 2 * BLOCK), jnp.float32),
            pltpu.VMEM((GROUP, 2 * BLOCK), jnp.float32),
            pltpu.VMEM((8, 2 * BLOCK), jnp.float32),
            pltpu.VMEM((HEAD_DIM, 2 * BLOCK), jnp.float32),
            pltpu.VMEM((GROUP, HEAD_DIM), jnp.float32),
            pltpu.VMEM((GROUP, HEAD_DIM), jnp.float32),
        ],
        compiler_params=PARAMS,
        name="attend",
    )(segments, most, arrived, extra, rows, cols)


def unpack(returned):
    return pl.pallas_call(
        unpack_kernel,
        out_shape=(shape((ROWS, 2048)), shape((ROWS, 1024)), shape((ROWS, 1024))),
        compiler_params=PARAMS,
        name="unpack",
    )(returned)


def relay(array):
    return lax.all_to_all(array, "dp", split_axis=0, concat_axis=0, tiled=True)


def local(query, key_rows, value_rows, attn_out, out_grad, source_row, segment_ids):
    me = lax.axis_index("seq").reshape(1)
    packed = pack(me, query, key_rows, value_rows, attn_out, out_grad)
    packed, source_row = lax.optimization_barrier((packed, source_row))
    parts = [packed[0]]
    for m in range(1, N_SEQ):
        parts.append(lax.ppermute(packed[m], "seq", [(s, s ^ m) for s in range(N_SEQ)]))
    pack_list = lax.all_gather(source_row, "seq", axis=0)
    rows, cols, request, most = index(pack_list, segment_ids)
    request = relay(request)
    arrived = relay(send(me, most, request, parts))
    extra = lax.cond(
        most[0, 0] >= CAPACITY,
        lambda request, *parts: relay(send_extra(me, request, parts)),
        lambda request, *parts: jnp.zeros((N_DP * EXTRA, WIDTH), jnp.bfloat16),
        request,
        *parts,
    )
    grads = attend(segment_ids, most, arrived, extra, rows, cols)
    returned = lax.all_to_all(
        grads.reshape(N_SEQ, ROWS, 4 * HEAD_DIM), "seq", split_axis=0, concat_axis=0, tiled=True
    )
    return unpack(returned)


def solution(mesh):
    in_specs = (
        P(("dp", "seq"), None),
        P(("dp", "seq"), None),
        P(("dp", "seq"), None),
        P(("dp", "seq"), None),
        P(("dp", "seq"), None),
        P(("dp", "seq")),
        P("dp"),
    )
    out_specs = (P(("dp", "seq"), None), P(("dp", "seq"), None), P(("dp", "seq"), None))
    return jax.shard_map(local, mesh=mesh, in_specs=in_specs, out_specs=out_specs, check_vma=False)
```

profile of v0, /device:TPU:1, one launch (start us, length us, event | category | flops | bytes accessed | tf_op | source)
XLA Modules:
  0.0 164.8 jit_solution(9648717084157805066)
XLA Ops:
  0.6 3.0 %pack.1 = (bf16[136,768]{1,0:T(8,128)(2,1)S(1)}, bf16[136,768]{1,0:T(8,128)(2,1)}, bf16[136,768]{1,0:T(8,128)(2,1)}, bf16[136,768]{1,0:T(8,128)(2,1)}, bf16[136,...) custom-call(s32[1]{0:T(128)} %bitcast.2.me_ref, ...), custom_call_target="tpu_custom_call" | custom-call | tf_op jit(solution)/shard_map/pack/pallas_call | solution.py:344
  3.6 3.3 %collective-permute-start = (bf16[136,768]{1,0:T(8,128)(2,1)}, bf16[136,768]{1,0:T(8,128)(2,1)S(1)}, u32[]{:S(2)}, u32[]{:S(2)}) collective-permute-start(bf16[136,768]{1,0:T(8,128)(2,1)} %get-tuple-element.69), channel_id=1, source_target_pairs={{0,1},{1,0},{2,3},{3,2},{4,5},{5,4},{6,7},{7,6},{8,9},{9,8},{10,11... | collective-permute-start | bytes 626696 | tf_op jit(solution)/shard_map/ppermute | solution.py:447
  7.0 0.0 collective-permute-start.1
  7.0 1.7 %collective-permute-start.2 = (bf16[136,768]{1,0:T(8,128)(2,1)}, bf16[136,768]{1,0:T(8,128)(2,1)S(1)}, u32[]{:S(2)}, u32[]{:S(2)}) collective-permute-start(bf16[136,768]{1,0:T(8,128)(2,1)} %get-tuple-element.71), channel_id=1, source_target_pairs={{0,3},{1,2},{2,1},{3,0},{4,7},{5,6},{6,5},{7,4},{8,11},{9,10},{10,... | collective-permute-start | bytes 626696 | tf_op jit(solution)/shard_map/ppermute | solution.py:447
  8.7 1.2 collective-permute-start.3
  9.9 2.1 %collective-permute-start.4 = (bf16[136,768]{1,0:T(8,128)(2,1)}, bf16[136,768]{1,0:T(8,128)(2,1)S(1)}, u32[]{:S(2)}, u32[]{:S(2)}) collective-permute-start(bf16[136,768]{1,0:T(8,128)(2,1)} %get-tuple-element.73), channel_id=1, source_target_pairs={{0,5},{1,4},{2,7},{3,6},{4,1},{5,0},{6,3},{7,2},{8,13},{9,12},{10,... | collective-permute-start | bytes 626696 | tf_op jit(solution)/shard_map/ppermute | solution.py:447
  12.0 0.0 collective-permute-done.refs_1_
  12.0 1.0 collective-permute-start.5
  13.0 0.9 collective-permute-done.1.refs_2_
  13.9 2.2 %collective-permute-start.6 = (bf16[136,768]{1,0:T(8,128)(2,1)}, bf16[136,768]{1,0:T(8,128)(2,1)S(1)}, u32[]{:S(2)}, u32[]{:S(2)}) collective-permute-start(bf16[136,768]{1,0:T(8,128)(2,1)} %get-tuple-element.75), channel_id=1, source_target_pairs={{0,7},{1,6},{2,5},{3,4},{4,3},{5,2},{6,1},{7,0},{8,15},{9,14},{10,... | collective-permute-start | bytes 626696 | tf_op jit(solution)/shard_map/ppermute | solution.py:447
  16.1 21.7 %all-gather.1 = s32[8,1,128]{2,1,0:T(1,128)S(1)} all-gather(s32[1,1,128]{2,1,0:T(1,128)} %bitcast.23), channel_id=2, replica_groups=mesh['dp'=32,'seq'=8] {'seq'}, dimensions={0}, use_global_device_ids=true | all-gather | bytes 4608 | tf_op jit(solution)/shard_map/all_gather | solution.py:448
  37.8 0.0 copy-start
  37.8 0.7 copy-done
  38.5 1.8 %index.1 = (f32[24,128]{1,0:T(8,128)S(1)}, f32[1024,128]{1,0:T(8,128)S(1)}, s32[32,128]{1,0:T(8,128)}, s32[1,1]{1,0:T(1,128)}) custom-call(s32[8,128]{1,0:T(8,128)S(1)} %bitcast.18, s32[8,128]{1,0:T(8,128)S(1)} %bitcast.19), custom_call_target="tpu_custom_call" | custom-call | tf_op jit(solution)/shard_map/index/pallas_call | solution.py:365
  40.3 11.0 %all-to-all-start.1 = ((s32[32,1,128]{2,1,0:T(1,128)}), s32[32,1,128]{2,1,0:T(1,128)S(1)}, u32[]{:S(2)}, u32[]{:S(2)}) async-start(s32[32,1,128]{2,1,0:T(1,128)} %bitcast.7), calls=%async_computation.1 | async-start | bytes 32768 | tf_op jit(solution)/shard_map/all_to_all | solution.py:438
  52.0 7.9 %all-to-all-done.1 = s32[32,1,128]{2,1,0:T(1,128)S(1)} async-done(((s32[32,1,128]{2,1,0:T(1,128)}), s32[32,1,128]{2,1,0:T(1,128)S(1)}, u32[]{:S(2)}, u32[]{:S(2)}) %all-to-all-start.1) | async-done | bytes 16416 | tf_op jit(solution)/shard_map/all_to_all | solution.py:438
  59.9 0.0 collective-permute-done.2.refs_3_
  59.9 0.0 collective-permute-done.3.refs_4_
  59.9 0.0 collective-permute-done.4.refs_5_
  59.9 0.0 collective-permute-done.5.refs_6_
  59.9 0.0 collective-permute-done.6.refs_7_
  59.9 0.1 conditional.1
  59.9 0.1 broadcast.2
  60.0 6.0 %send.1 = bf16[1792,768]{1,0:T(8,128)(2,1)S(1)} custom-call(s32[1]{0:T(128)} %bitcast.2.me_ref, s32[1,1]{1,0:T(1,128)} %get-tuple-element.66.most_ref, s32[32,128]{1,0:T(8,128)S(1)} %bitcast.22, bf16[136,768]{1,0:T(8,128)(2,1)S(1)} %get-tuple-element.68.refs_0_, bf16[136,768]{1,0:T(8,128)(2,1)S(1)} %collective-permute-done.refs_1_, ...), custom_call_target="tpu_custom_call" | custom-call | flops 2818572288 | bytes 4000000 | tf_op jit(solution)/shard_map/send/pallas_call | solution.py:380
  66.0 0.0 copy-start.1
  66.0 66.0 %all_to_all.37 = bf16[32,56,768]{2,1,0:T(8,128)(2,1)S(1)} all-to-all(bf16[32,56,768]{2,1,0:T(8,128)(2,1)S(1)} %bitcast.17), channel_id=1, replica_groups=mesh['dp'=32,'seq'=8] {'dp'}, dimensions={0} | all-to-all | bytes 5505024 | tf_op jit(solution)/shard_map/all_to_all | solution.py:438
  132.1 0.0 copy-done.1
  132.1 10.9 %attend.1 = bf16[1024,512]{1,0:T(8,128)(2,1)S(1)} custom-call(s32[1024]{0:T(1024)S(1)} %copy-done.1, s32[1,1]{1,0:T(1,128)} %get-tuple-element.66.most_ref, bf16[1792,768]{1,0:T(8,128)(2,1)S(1)} %bitcast.14, bf16[512,768]{1,0:T(8,128)(2,1)S(1)} %get-tuple-element.78.extra_ref, f32[24,128]{1,0:T(8,128)S(1)} %get-tuple-element.76.rows_ref, ...), custom_call_target="tpu_custom_call" | custom-call | tf_op jit(solution)/shard_map/attend/pallas_call | solution.py:408
  143.0 20.7 %all_to_all.38.returned_ref = bf16[8,128,512]{2,1,0:T(8,128)(2,1)S(1)} all-to-all(bf16[8,128,512]{2,1,0:T(8,128)(2,1)S(1)} %bitcast.15), channel_id=1, replica_groups=mesh['dp'=32,'seq'=8] {'seq'}, dimensions={0} | all-to-all | bytes 2097152 | tf_op jit(solution)/shard_map/all_to_all | solution.py:460
  163.7 1.2 unpack.1
Async XLA Ops:
  3.6 8.4 %collective-permute-start = (bf16[136,768]{1,0:T(8,128)(2,1)}, bf16[136,768]{1,0:T(8,128)(2,1)S(1)}, u32[]{:S(2)}, u32[]{:S(2)}) collective-permute-start(bf16[136,768]{1,0:T(8,128)(2,1)} %get-tuple-element.69), channel_id=1, source_target_pairs={{0,1},{1,0},{2,3},{3,2},{4,5},{5,4},{6,7},{7,6},{8,9},{9,8},{10,11... | collective-permute-start | bytes 626696 | tf_op jit(solution)/shard_map/ppermute | solution.py:447
  7.0 6.9 %collective-permute-start.1 = (bf16[136,768]{1,0:T(8,128)(2,1)}, bf16[136,768]{1,0:T(8,128)(2,1)S(1)}, u32[]{:S(2)}, u32[]{:S(2)}) collective-permute-start(bf16[136,768]{1,0:T(8,128)(2,1)} %get-tuple-element.70), channel_id=1, source_target_pairs={{0,2},{1,3},{2,0},{3,1},{4,6},{5,7},{6,4},{7,5},{8,10},{9,11},{10,... | collective-permute-start | bytes 626696 | tf_op jit(solution)/shard_map/ppermute | solution.py:447
  7.0 52.9 %collective-permute-start.2 = (bf16[136,768]{1,0:T(8,128)(2,1)}, bf16[136,768]{1,0:T(8,128)(2,1)S(1)}, u32[]{:S(2)}, u32[]{:S(2)}) collective-permute-start(bf16[136,768]{1,0:T(8,128)(2,1)} %get-tuple-element.71), channel_id=1, source_target_pairs={{0,3},{1,2},{2,1},{3,0},{4,7},{5,6},{6,5},{7,4},{8,11},{9,10},{10,... | collective-permute-start | bytes 626696 | tf_op jit(solution)/shard_map/ppermute | solution.py:447
  8.7 51.2 %collective-permute-start.3 = (bf16[136,768]{1,0:T(8,128)(2,1)}, bf16[136,768]{1,0:T(8,128)(2,1)S(1)}, u32[]{:S(2)}, u32[]{:S(2)}) collective-permute-start(bf16[136,768]{1,0:T(8,128)(2,1)} %get-tuple-element.72), channel_id=1, source_target_pairs={{0,4},{1,5},{2,6},{3,7},{4,0},{5,1},{6,2},{7,3},{8,12},{9,13},{10,... | collective-permute-start | bytes 626696 | tf_op jit(solution)/shard_map/ppermute | solution.py:447
  9.9 50.0 %collective-permute-start.4 = (bf16[136,768]{1,0:T(8,128)(2,1)}, bf16[136,768]{1,0:T(8,128)(2,1)S(1)}, u32[]{:S(2)}, u32[]{:S(2)}) collective-permute-start(bf16[136,768]{1,0:T(8,128)(2,1)} %get-tuple-element.73), channel_id=1, source_target_pairs={{0,5},{1,4},{2,7},{3,6},{4,1},{5,0},{6,3},{7,2},{8,13},{9,12},{10,... | collective-permute-start | bytes 626696 | tf_op jit(solution)/shard_map/ppermute | solution.py:447
  12.0 47.9 %collective-permute-start.5 = (bf16[136,768]{1,0:T(8,128)(2,1)}, bf16[136,768]{1,0:T(8,128)(2,1)S(1)}, u32[]{:S(2)}, u32[]{:S(2)}) collective-permute-start(bf16[136,768]{1,0:T(8,128)(2,1)} %get-tuple-element.74), channel_id=1, source_target_pairs={{0,6},{1,7},{2,4},{3,5},{4,2},{5,3},{6,0},{7,1},{8,14},{9,15},{10,... | collective-permute-start | bytes 626696 | tf_op jit(solution)/shard_map/ppermute | solution.py:447
  13.9 46.0 %collective-permute-start.6 = (bf16[136,768]{1,0:T(8,128)(2,1)}, bf16[136,768]{1,0:T(8,128)(2,1)S(1)}, u32[]{:S(2)}, u32[]{:S(2)}) collective-permute-start(bf16[136,768]{1,0:T(8,128)(2,1)} %get-tuple-element.75), channel_id=1, source_target_pairs={{0,7},{1,6},{2,5},{3,4},{4,3},{5,2},{6,1},{7,0},{8,15},{9,14},{10,... | collective-permute-start | bytes 626696 | tf_op jit(solution)/shard_map/ppermute | solution.py:447
  37.8 0.7 copy-start
  40.3 19.6 %all-to-all-start.1 = ((s32[32,1,128]{2,1,0:T(1,128)}), s32[32,1,128]{2,1,0:T(1,128)S(1)}, u32[]{:S(2)}, u32[]{:S(2)}) async-start(s32[32,1,128]{2,1,0:T(1,128)} %bitcast.7), calls=%async_computation.1 | async-start | bytes 32768 | tf_op jit(solution)/shard_map/all_to_all | solution.py:438
  66.0 66.1 %copy-start.1 = (s32[1024]{0:T(1024)S(1)}, s32[1024]{0:T(1024)}, u32[]{:S(2)}) copy-start(s32[1024]{0:T(1024)} %segment_ref.1) | copy-start | bytes 12292
where the time goes:
time: 165 us
  blocking collectives  108 us (65%)
  Pallas kernels  22.9 us (14%)
  starting transfers between devices  22.6 us (14%)
  waiting for transfers between devices  8.78 us (5%)
    all_to_all x1, blocking collectives, relay(): return lax.all_to_all(array, 'dp', split_axis=0, concat_axis=0, tiled=True)  66 us
    all_gather x1, blocking collectives, local(): pack_list = lax.all_gather(source_row, 'seq', axis=0)  21.7 us
    all_to_all x1, blocking collectives, local(): lax.all_to_all(grads.reshape(N_SEQ, ROWS, 4 * HEAD_DIM), 'seq', split_axi...  20.7 us
    ppermute x7, starting transfers between devices, local(): lax.ppermute(packed[m], 'seq', [(s, s ^ m) for s in range(N_SEQ)])  11.6 us
    all_to_all x1, starting transfers between devices, relay(): return lax.all_to_all(array, 'dp', split_axis=0, concat_axis=0, tiled=True)  11 us
    pallas_call x1, Pallas kernels, attend(): pl.pallas_call(attend_kernel, out_shape=shape((GROUP, 4 * HEAD_DIM)), in_...  10.9 us
    all_to_all x1, waiting for transfers between devices, relay(): return lax.all_to_all(array, 'dp', split_axis=0, concat_axis=0, tiled=True)  7.86 us
    pallas_call x1, Pallas kernels, send(): pl.pallas_call(send_kernel, out_shape=shape((N_DP * CAPACITY, WIDTH)), in...  5.99 us
  transfers between devices with their start and end apart: 8, of which 2 were waited for; matrix products, arithmetic and copies ran while one was open for 0% of the time, Pallas kernels for 1%

commit v1 on v0

--- a/solution.py
+++ b/solution.py
@@ -90,7 +90,10 @@
     return jnp.concatenate([rows[s : s + 1] for s in range(N_SEQ)], axis=1)
 
 
-def index_kernel(list_ref, segment_ref, rows_ref, cols_ref, request_ref, most_ref):
+def index_kernel(me_ref, segment_ref, *refs):
+    lists, (rows_ref, cols_ref, request_ref, most_ref, list_ref) = refs[:N_SEQ], refs[N_SEQ:]
+    for m in range(N_SEQ):
+        list_ref[pl.ds(jnp.bitwise_xor(me_ref[0], m), 1), :] = lists[m][...]
     listed = list_ref[...]
     source = (listed // GROUP).astype(jnp.float32)
     local_row = (listed % ROWS).astype(jnp.float32)
@@ -129,19 +132,19 @@
     most_ref[0, 0] = (jnp.max(slot) + 1.0).astype(jnp.int32)
 
 
-def request_picks(turned, group, first, capacity, width):
-    column = jnp.concatenate(
-        [turned[first : first + capacity, d : d + 1] for d in range(8 * group, 8 * group + 8)], axis=0
-    )
-    row_id = iota((8 * capacity, width), 1).astype(jnp.float32)
+def spread_requests(request_ref, first, capacity, column_ref):
+    blank = jnp.zeros((LANES - N_DP, LANES), jnp.float32)
+    turned = jnp.concatenate([request_ref[...].astype(jnp.float32), blank], axis=0).T - 1.0
+    for owner in range(N_DP):
+        column_ref[owner * capacity : (owner + 1) * capacity, :] = jnp.broadcast_to(
+            turned[first : first + capacity, owner : owner + 1], (capacity, LANES)
+        )
+
+
+def group_picks(column_ref, group, group_rows):
+    column = column_ref[pl.ds(pl.multiple_of(group * group_rows, group_rows), group_rows), 0:1]
+    row_id = iota((group_rows, GROUP), 1).astype(jnp.float32)
     return (column == row_id).astype(jnp.float32).astype(jnp.bfloat16)
-
-
-def turned_requests(request_ref):
-    blank = jnp.zeros((LANES - N_DP, LANES), jnp.float32)
-    turned = jnp.concatenate([request_ref[...].astype(jnp.float32), blank], axis=0).T
-    delta_id = (iota((LANES, LANES), 1) + GROUP).astype(jnp.float32)
-    return jnp.where(iota((LANES, LANES), 0) == 0, delta_id, turned - 1.0)
 
 
 def join_columns(me_ref, parts, ext_ref, delta_ref):
@@ -153,46 +156,55 @@
 
 
 def send_extra_kernel(me_ref, request_ref, *refs):
-    parts, (sent_ref, ext_ref) = refs[:N_SEQ], refs[N_SEQ:]
+    parts, (sent_ref, ext_ref, column_ref) = refs[:N_SEQ], refs[N_SEQ:]
     group_rows = 8 * EXTRA
-    turned = turned_requests(request_ref)
+    spread_requests(request_ref, CAPACITY, EXTRA, column_ref)
     join_columns(me_ref, parts, ext_ref, None)
-    for group in range(N_DP // 8):
-        pick = request_picks(turned, group, CAPACITY, EXTRA, GROUP)
-        rows = slice(group * group_rows, (group + 1) * group_rows)
+
+    def fill(group, carry):
+        pick = group_picks(column_ref, group, group_rows)
+        rows = pl.ds(pl.multiple_of(group * group_rows, group_rows), group_rows)
         sent_ref[rows, :] = nn_dot(pick, ext_ref[...]).astype(jnp.bfloat16)
+        return carry
+
+    lax.fori_loop(0, N_DP // 8, fill, 0)
 
 
 def send_kernel(me_ref, most_ref, request_ref, *refs):
-    parts, (sent_ref, pick_ref, ext_ref, place_ref, delta_ref) = refs[:N_SEQ], refs[N_SEQ:]
+    parts = refs[:N_SEQ]
+    sent_ref, pick_ref, ext_ref, column_ref, place_ref, delta_ref, tail_ref, more_ref = refs[N_SEQ:]
     capacity = CAPACITY
     group_rows = 8 * capacity
-    turned = turned_requests(request_ref)
+    spread_requests(request_ref, 0, capacity, column_ref)
     join_columns(me_ref, parts, ext_ref, delta_ref)
     delta = jnp.concatenate([delta_ref[s] for s in range(N_SEQ)], axis=1)
-
-    def places(pick, group, first, count):
+    place_ref[...] = jnp.zeros_like(place_ref)
+
+    def add_places(pick, group, first, count):
         index = iota((8, 8 * count), 1)
         owner = index // count
         value = jnp.where(
             iota((8, 8 * count), 0) == 0, owner + 8 * group, index - owner * count + first
         )
-        return nn_dot(value.astype(jnp.float32).astype(jnp.bfloat16), pick[:, :GROUP])
-
-    place = jnp.zeros((8, GROUP), jnp.float32)
-    for group in range(N_DP // 8):
-        pick = request_picks(turned, group, 0, capacity, GROUP + LANES)
-        pick_ref[group * group_rows : (group + 1) * group_rows, :] = pick
-        place = place + places(pick, group, 0, capacity)
-    place_ref[...] = place
+        place_ref[...] += nn_dot(value.astype(jnp.float32).astype(jnp.bfloat16), pick)
+
+    def pick_group(group, carry):
+        pick = group_picks(column_ref, group, group_rows)
+        pick_ref[pl.ds(pl.multiple_of(group * group_rows, group_rows), group_rows), :] = pick
+        add_places(pick, group, 0, capacity)
+        return carry
+
+    lax.fori_loop(0, N_DP // 8, pick_group, 0)
 
     @pl.when(most_ref[0, 0] >= CAPACITY)
     def _():
-        more = jnp.zeros((8, GROUP), jnp.float32)
-        for group in range(N_DP // 8):
-            pick = request_picks(turned, group, CAPACITY, EXTRA, GROUP)
-            more = more + places(pick, group, CAPACITY, EXTRA)
-        place_ref[...] += more
+        spread_requests(request_ref, CAPACITY, EXTRA, more_ref)
+
+        def pick_more(group, carry):
+            add_places(group_picks(more_ref, group, 8 * EXTRA), group, CAPACITY, EXTRA)
+            return carry
+
+        lax.fori_loop(0, N_DP // 8, pick_more, 0)
 
     place = place_ref[...]
     owner_of = place[0:1]
@@ -211,49 +223,70 @@
         )
         slot_pick = (slot_col + (64.0 * head - 1.0) == lane).astype(jnp.float32)
         tail = tail + nn_dot(spread.astype(jnp.bfloat16), slot_pick.astype(jnp.bfloat16))
-    tail = jnp.concatenate(
-        [tail[:N_DP], tail[N_DP:], jnp.zeros((N_DP, WIDTH - 2 * LANES), jnp.float32)], axis=1
-    )
-    tail = jnp.concatenate([tail, jnp.zeros((LANES - N_DP, WIDTH), jnp.float32)], axis=0)
-    ext_ref[GROUP:, :] = tail.astype(jnp.bfloat16)
-    for group in range(N_DP // 8):
-        rows = slice(group * group_rows, (group + 1) * group_rows)
-        sent_ref[rows, :] = nn_dot(pick_ref[rows, :], ext_ref[...]).astype(jnp.bfloat16)
+    tail_ref[...] = jnp.concatenate([tail[:N_DP], tail[N_DP:]], axis=1)
+
+    def fill(group, carry):
+        rows = pl.ds(pl.multiple_of(group * group_rows, group_rows), group_rows)
+        sent = nn_dot(pick_ref[rows, :], ext_ref[...])
+        tails = tail_ref[pl.ds(pl.multiple_of(8 * group, 8), 8), :]
+        tails = jnp.concatenate(
+            [jnp.broadcast_to(tails[j : j + 1], (capacity, 2 * LANES)) for j in range(8)], axis=0
+        )
+        index = iota((group_rows, 2 * LANES), 0)
+        left = jnp.where(index % capacity == 0, tails, sent[:, : 2 * LANES])
+        sent_ref[rows, : 2 * LANES] = left.astype(jnp.bfloat16)
+        sent_ref[rows, 2 * LANES :] = sent[:, 2 * LANES :].astype(jnp.bfloat16)
+        return carry
+
+    lax.fori_loop(0, N_DP // 8, fill, 0)
 
 
 def attend_kernel(
     segment_ref, most_ref, arrived_ref, extra_ref, rows_ref, cols_ref, out_ref,
-    x_ref, kt_ref, delta_ref, weight_ref, squash_ref, total_ref, gqt_ref, gk_ref, gv_ref,
+    x_ref, kt_ref, lanes_ref, query_ref, grad_ref, weight_ref, squash_ref, total_ref, gqt_ref,
+    gk_ref, gv_ref,
 ):
     slots = N_DP * CAPACITY
     blocks = GROUP // BLOCK
-    slot_id = iota((BLOCK, slots), 1).astype(jnp.float32)
-    for block in range(blocks):
-        rows = slice(block * BLOCK, (block + 1) * BLOCK)
+
+    def span(block):
+        return pl.ds(pl.multiple_of(block * BLOCK, BLOCK), BLOCK)
+
+    def gather(block, carry):
+        rows = span(block)
+        slot_id = iota((BLOCK, slots), 1).astype(jnp.float32)
         slot = cols_ref[rows, 1:2] + 1.0
         place = jnp.where(slot < CAPACITY, cols_ref[rows, 0:1] * float(CAPACITY) + slot, -1.0)
         pick = (place == slot_id).astype(jnp.float32).astype(jnp.bfloat16)
         x_ref[rows, :] = nn_dot(pick, arrived_ref[...]).astype(jnp.bfloat16)
+        return carry
+
+    def gather_extra(block, carry):
+        rows = span(block)
+        extra_id = iota((BLOCK, N_DP * EXTRA), 1).astype(jnp.float32)
+        slot = cols_ref[rows, 1:2] - float(CAPACITY - 1)
+        place = jnp.where(slot >= 0.0, cols_ref[rows, 0:1] * float(EXTRA) + slot, -1.0)
+        pick = (place == extra_id).astype(jnp.float32).astype(jnp.bfloat16)
+        x_ref[rows, :] += nn_dot(pick, extra_ref[...]).astype(jnp.bfloat16)
+        return carry
+
+    def turn_keys(block, carry):
+        rows = span(block)
+        kt_ref[:, rows] = x_ref[rows, 256:384].astype(jnp.float32).T.astype(jnp.bfloat16)
+        return carry
+
+    lax.fori_loop(0, blocks, gather, 0)
 
     @pl.when(most_ref[0, 0] >= CAPACITY)
     def _():
-        extra_id = iota((BLOCK, N_DP * EXTRA), 1).astype(jnp.float32)
-        for block in range(blocks):
-            rows = slice(block * BLOCK, (block + 1) * BLOCK)
-            slot = cols_ref[rows, 1:2] - float(CAPACITY - 1)
-            place = jnp.where(slot >= 0.0, cols_ref[rows, 0:1] * float(EXTRA) + slot, -1.0)
-            pick = (place == extra_id).astype(jnp.float32).astype(jnp.bfloat16)
-            x_ref[rows, :] += nn_dot(pick, extra_ref[...]).astype(jnp.bfloat16)
-
-    for block in range(blocks):
-        rows = slice(block * BLOCK, (block + 1) * BLOCK)
-        kt_ref[:, rows] = x_ref[rows, 256:384].astype(jnp.float32).T.astype(jnp.bfloat16)
+        lax.fori_loop(0, blocks, gather_extra, 0)
+
+    lax.fori_loop(0, blocks, turn_keys, 0)
     first = iota((LANES, slots), 0) * CAPACITY == iota((LANES, slots), 1)
     first = first.astype(jnp.float32).astype(jnp.bfloat16)
     parts = nn_dot(first, arrived_ref[:, : 2 * LANES])
     source = wide(rows_ref[0:8, :])
     slot = wide(rows_ref[8:16, :])
-    segment = wide(rows_ref[16:24, :])
     from_source = iota((LANES, GROUP), 0).astype(jnp.float32) == source
     from_source = from_source.astype(jnp.float32).astype(jnp.bfloat16)
     high = parts[:, :LANES].T.astype(jnp.bfloat16)
@@ -261,60 +294,63 @@
     both = nn_dot(high, from_source) + nn_dot(low, from_source)
     place = iota((LANES, GROUP), 0).astype(jnp.float32)
     for head in range(2):
-        delta_ref[head : head + 1, :] = jnp.sum(
+        lanes_ref[head : head + 1, :] = jnp.sum(
             jnp.where(place == slot + 64.0 * head, both, 0.0), axis=0, keepdims=True
         )
+    lanes_ref[2:3, :] = wide(rows_ref[16:24, :])
     gk_ref[...] = jnp.zeros_like(gk_ref)
     gv_ref[...] = jnp.zeros_like(gv_ref)
-    causal = iota((BLOCK, BLOCK), 0) <= iota((BLOCK, BLOCK), 1)
-    causal = jnp.concatenate([causal.astype(jnp.float32)] * 2, axis=1) > 0.0
-    for block in range(blocks):
-        rows = slice(block * BLOCK, (block + 1) * BLOCK)
-        queries = jnp.concatenate([x_ref[rows, 0:128], x_ref[rows, 128:256]], axis=0)
-        grads = jnp.concatenate([x_ref[rows, 512:640], x_ref[rows, 640:768]], axis=0)
-        delta = jnp.concatenate([delta_ref[0:1, rows], delta_ref[1:2, rows]], axis=1)
-        segment_q = jnp.concatenate([segment[:, rows]] * 2, axis=1)
-
-        def weigh(key_block):
-            keys = slice(key_block * BLOCK, (key_block + 1) * BLOCK)
-            score = nt_dot(x_ref[keys, 256:384], queries)
+
+    def attend_block(block, carry):
+        rows = span(block)
+        query_ref[:BLOCK, :] = x_ref[rows, 0:128]
+        query_ref[BLOCK:, :] = x_ref[rows, 128:256]
+        grad_ref[:BLOCK, :] = x_ref[rows, 512:640]
+        grad_ref[BLOCK:, :] = x_ref[rows, 640:768]
+        total_ref[...] = jnp.zeros_like(total_ref)
+        gqt_ref[...] = jnp.zeros_like(gqt_ref)
+        first_segment = segment_ref[block * BLOCK]
+        start = jnp.int32(0)
+        for key_block in range(blocks - 1):
+            ends = segment_ref[(key_block + 1) * BLOCK - 1] < first_segment
+            start = start + jnp.where(ends & (key_block < block), 1, 0)
+
+        def weigh(key_block, carry):
+            keys = span(key_block)
+            score = nt_dot(x_ref[keys, 256:384], query_ref[...])
             squashed = jnp.tanh(score * (scaling / softcap))
-            allowed = cols_ref[keys, 2:3] == segment_q
-            if key_block == block:
-                allowed = allowed & causal
+            segment_q = jnp.concatenate([lanes_ref[2:3, rows]] * 2, axis=1)
+            ahead = iota((BLOCK, BLOCK), 0) - iota((BLOCK, BLOCK), 1)
+            ahead = jnp.concatenate([ahead, ahead], axis=1)
+            allowed = (cols_ref[keys, 2:3] == segment_q) & (ahead <= (block - key_block) * BLOCK)
             weights = jnp.where(allowed, jnp.exp(softcap * squashed), 0.0)
             weight_ref[keys, :] = weights
             squash_ref[keys, :] = squashed
-            total = jnp.sum(weights, axis=0, keepdims=True)
-            if key_block == block:
-                total_ref[0:1, :] = total
-            else:
-                total_ref[0:1, :] += total
-
-        def back(key_block):
-            keys = slice(key_block * BLOCK, (key_block + 1) * BLOCK)
-            probabilities = weight_ref[keys, :] * (1.0 / total_ref[0:1, :])
-            gv_ref[keys, :] += nn_dot(probabilities.astype(jnp.bfloat16), grads)
-            prob_grad = nt_dot(x_ref[keys, 384:512], grads)
+            total_ref[0:1, :] += jnp.sum(weights, axis=0, keepdims=True)
+            return carry
+
+        def back(key_block, carry):
+            keys = span(key_block)
+            delta = jnp.concatenate([lanes_ref[0:1, rows], lanes_ref[1:2, rows]], axis=1)
+            probabilities = weight_ref[keys, :] * total_ref[0:1, :]
+            gv_ref[keys, :] += nn_dot(probabilities.astype(jnp.bfloat16), grad_ref[...])
+            prob_grad = nt_dot(x_ref[keys, 384:512], grad_ref[...])
             squashed = squash_ref[keys, :]
             score_grad = probabilities * (prob_grad - delta) * (1.0 - squashed * squashed)
             score_grad = score_grad.astype(jnp.bfloat16)
-            gk_ref[keys, :] += nn_dot(score_grad, queries)
-            part = nn_dot(kt_ref[:, keys], score_grad)
-            if key_block == block:
-                gqt_ref[...] = part
-            else:
-                gqt_ref[...] += part
-
-        first_segment = segment_ref[block * BLOCK]
-        for step in (weigh, back):
-            step(block)
-            for key_block in range(block):
-                meets = segment_ref[(key_block + 1) * BLOCK - 1] == first_segment
-                pl.when(meets)(functools.partial(step, key_block))
+            gk_ref[keys, :] += nn_dot(score_grad, query_ref[...])
+            gqt_ref[...] += nn_dot(kt_ref[:, keys], score_grad)
+            return carry
+
+        lax.fori_loop(start, block + 1, weigh, 0)
+        total_ref[...] = 1.0 / total_ref[...]
+        lax.fori_loop(start, block + 1, back, 0)
         turned = (gqt_ref[...].T * scaling).astype(jnp.bfloat16)
         out_ref[rows, 0:128] = turned[:BLOCK]
         out_ref[rows, 128:256] = turned[BLOCK:]
+        return carry
+
+    lax.fori_loop(0, blocks, attend_block, 0)
     out_ref[:, 256:384] = (gk_ref[...] * scaling).astype(jnp.bfloat16)
     out_ref[:, 384:512] = gv_ref[...].astype(jnp.bfloat16)
 
@@ -360,8 +396,7 @@
     )(me, query, key_rows, value_rows, attn_out, out_grad)
 
 
-def index(pack_list, segments):
-    vmem = pl.BlockSpec(memory_space=pltpu.VMEM)
+def index(me, segments, lists):
     return pl.pallas_call(
         index_kernel,
         out_shape=(
@@ -370,10 +405,12 @@
             shape((N_DP, LANES), jnp.int32),
             shape((1, 1), jnp.int32),
         ),
-        out_specs=(vmem, vmem, vmem, pl.BlockSpec(memory_space=pltpu.SMEM)),
+        in_specs=[SMEM] + [VMEM] * 9,
+        out_specs=(VMEM, VMEM, VMEM, SMEM),
+        scratch_shapes=[pltpu.VMEM((N_SEQ, LANES), jnp.int32)],
         compiler_params=PARAMS,
         name="index",
-    )(pack_list, segments.reshape(N_SEQ, ROWS))
+    )(me, segments.reshape(N_SEQ, ROWS), *lists)
 
 
 def send(me, most, request, parts):
@@ -382,10 +419,13 @@
         out_shape=shape((N_DP * CAPACITY, WIDTH)),
         in_specs=[SMEM, SMEM] + [VMEM] * 9,
         scratch_shapes=[
-            pltpu.VMEM((N_DP * CAPACITY, GROUP + LANES), jnp.bfloat16),
-            pltpu.VMEM((GROUP + LANES, WIDTH), jnp.bfloat16),
+            pltpu.VMEM((N_DP * CAPACITY, GROUP), jnp.bfloat16),
+            pltpu.VMEM((GROUP, WIDTH), jnp.bfloat16),
+            pltpu.VMEM((N_DP * CAPACITY, LANES), jnp.float32),
             pltpu.VMEM((8, GROUP), jnp.float32),
             pltpu.VMEM((N_SEQ, 8, LANES), jnp.float32),
+            pltpu.VMEM((N_DP, 2 * LANES), jnp.float32),
+            pltpu.VMEM((N_DP * EXTRA, LANES), jnp.float32),
         ],
         compiler_params=PARAMS,
         cost_estimate=cost(2 * N_DP * CAPACITY * GROUP * WIDTH, 4_000_000),
@@ -398,7 +438,10 @@
         send_extra_kernel,
         out_shape=shape((N_DP * EXTRA, WIDTH)),
         in_specs=[SMEM] + [VMEM] * 9,
-        scratch_shapes=[pltpu.VMEM((GROUP, WIDTH), jnp.bfloat16)],
+        scratch_shapes=[
+            pltpu.VMEM((GROUP, WIDTH), jnp.bfloat16),
+            pltpu.VMEM((N_DP * EXTRA, LANES), jnp.float32),
+        ],
         compiler_params=PARAMS,
         name="send_extra",
     )(me, request, *parts)
@@ -413,6 +456,8 @@
             pltpu.VMEM((GROUP, WIDTH), jnp.bfloat16),
             pltpu.VMEM((HEAD_DIM, GROUP), jnp.bfloat16),
             pltpu.VMEM((8, GROUP), jnp.float32),
+            pltpu.VMEM((2 * BLOCK, HEAD_DIM), jnp.bfloat16),
+            pltpu.VMEM((2 * BLOCK, HEAD_DIM), jnp.bfloat16),
             pltpu.VMEM((GROUP, 2 * BLOCK), jnp.float32),
             pltpu.VMEM((GROUP, 2 * BLOCK), jnp.float32),
             pltpu.VMEM((8, 2 * BLOCK), jnp.float32),
@@ -440,13 +485,15 @@
 
 def local(query, key_rows, value_rows, attn_out, out_grad, source_row, segment_ids):
     me = lax.axis_index("seq").reshape(1)
+
+    def swap(array, m):
+        return lax.ppermute(array, "seq", [(s, s ^ m) for s in range(N_SEQ)]) if m else array
+
+    lists = [swap(source_row.reshape(1, ROWS), m) for m in range(N_SEQ)]
     packed = pack(me, query, key_rows, value_rows, attn_out, out_grad)
-    packed, source_row = lax.optimization_barrier((packed, source_row))
-    parts = [packed[0]]
-    for m in range(1, N_SEQ):
-        parts.append(lax.ppermute(packed[m], "seq", [(s, s ^ m) for s in range(N_SEQ)]))
-    pack_list = lax.all_gather(source_row, "seq", axis=0)
-    rows, cols, request, most = index(pack_list, segment_ids)
+    packed, lists = lax.optimization_barrier((packed, lists))
+    parts = [swap(packed[m], m) for m in range(N_SEQ)]
+    rows, cols, request, most = index(me, segment_ids, lists)
     request = relay(request)
     arrived = relay(send(me, most, request, parts))
     extra = lax.cond(

time: 165 us -> 158 us (0.958)
  blocking collectives: 108 us -> 88.9 us
  starting transfers between devices: 22.6 us -> 30.9 us
  Pallas kernels: 22.9 us -> 26.5 us
    all_gather x1 -> x0, blocking collectives: 21.7 us -> none  [local(): pack_list = lax.all_gather(source_row, 'seq', axis=0)]
    ppermute x7 -> x14, starting transfers between devices: 11.6 us -> 19.8 us  [swap(): lax.ppermute(array, 'seq', [(s, s ^ m) for s in range(N_SEQ)])]
    all_to_all x1, blocking collectives: 66 us -> 68.8 us  [relay(): return lax.all_to_all(array, 'dp', split_axis=0, concat_axis=0, tiled=True)]
    pallas_call x1, Pallas kernels: 10.9 us -> 13.5 us  [attend(): pl.pallas_call(attend_kernel, out_shape=shape((GROUP, 4 * HEAD_DIM)), in_...]
  transfers between devices with their start and end apart: 8 -> 15, of which waited for: 2 -> 2; matrix products, arithmetic and copies ran while one was open for 0% -> 0% of each run, Pallas kernels for 1% -> 3%
where the time goes in v1:
time: 158 us
  blocking collectives  88.9 us (56%)
  starting transfers between devices  30.9 us (20%)
  Pallas kernels  26.5 us (17%)
  waiting for transfers between devices  8.85 us (6%)
    all_to_all x1, blocking collectives, relay(): return lax.all_to_all(array, 'dp', split_axis=0, concat_axis=0, tiled=True)  68.8 us
    all_to_all x1, blocking collectives, local(): lax.all_to_all(grads.reshape(N_SEQ, ROWS, 4 * HEAD_DIM), 'seq', split_axi...  20.2 us
    ppermute x14, starting transfers between devices, swap(): lax.ppermute(array, 'seq', [(s, s ^ m) for s in range(N_SEQ)])  19.8 us
    pallas_call x1, Pallas kernels, attend(): pl.pallas_call(attend_kernel, out_shape=shape((GROUP, 4 * HEAD_DIM)), in_...  13.5 us
    all_to_all x1, starting transfers between devices, relay(): return lax.all_to_all(array, 'dp', split_axis=0, concat_axis=0, tiled=True)  11 us
    all_to_all x1, waiting for transfers between devices, relay(): return lax.all_to_all(array, 'dp', split_axis=0, concat_axis=0, tiled=True)  7.95 us
    pallas_call x1, Pallas kernels, send(): pl.pallas_call(send_kernel, out_shape=shape((N_DP * CAPACITY, WIDTH)), in...  6.99 us
  transfers between devices with their start and end apart: 15, of which 2 were waited for; matrix products, arithmetic and copies ran while one was open for 0% of the time, Pallas kernels for 3%

profile of v1, /device:TPU:1, one launch (start us, length us, event | category | flops | bytes accessed | tf_op | source)
XLA Modules:
  0.0 157.9 jit_solution(2529656407662754454)
XLA Ops:
  0.6 4.2 %collective-permute-start.6 = (s32[1,128]{1,0:T(1,128)}, s32[1,128]{1,0:T(1,128)S(1)}, u32[]{:S(2)}, u32[]{:S(2)}) collective-permute-start(s32[1,128]{1,0:T(1,128)} %bitcast.18), channel_id=1, source_target_pairs={{0,7},{1,6},{2,5},{3,4},{4,3},{5,2},{6,1},{7,0},{8,15},{9,14},{10,... | collective-permute-start | bytes 1544 | tf_op jit(solution)/shard_map/ppermute | solution.py:490
  4.8 1.7 %collective-permute-start.5 = (s32[1,128]{1,0:T(1,128)}, s32[1,128]{1,0:T(1,128)S(1)}, u32[]{:S(2)}, u32[]{:S(2)}) collective-permute-start(s32[1,128]{1,0:T(1,128)} %bitcast.19), channel_id=1, source_target_pairs={{0,6},{1,7},{2,4},{3,5},{4,2},{5,3},{6,0},{7,1},{8,14},{9,15},{10,... | collective-permute-start | bytes 1544 | tf_op jit(solution)/shard_map/ppermute | solution.py:490
  6.5 0.0 collective-permute-start.4
  6.5 1.7 %collective-permute-start.3 = (s32[1,128]{1,0:T(1,128)}, s32[1,128]{1,0:T(1,128)S(1)}, u32[]{:S(2)}, u32[]{:S(2)}) collective-permute-start(s32[1,128]{1,0:T(1,128)} %bitcast.21), channel_id=1, source_target_pairs={{0,4},{1,5},{2,6},{3,7},{4,0},{5,1},{6,2},{7,3},{8,12},{9,13},{10,... | collective-permute-start | bytes 1544 | tf_op jit(solution)/shard_map/ppermute | solution.py:490
  8.2 0.3 collective-permute-start.2
  8.4 0.0 collective-permute-done.6.refs_7_
  8.5 3.1 %collective-permute-start.1 = (s32[1,128]{1,0:T(1,128)}, s32[1,128]{1,0:T(1,128)S(1)}, u32[]{:S(2)}, u32[]{:S(2)}) collective-permute-start(s32[1,128]{1,0:T(1,128)} %bitcast.23), channel_id=1, source_target_pairs={{0,2},{1,3},{2,0},{3,1},{4,6},{5,7},{6,4},{7,5},{8,10},{9,11},{10,... | collective-permute-start | bytes 1544 | tf_op jit(solution)/shard_map/ppermute | solution.py:490
  11.5 0.0 collective-permute-done.5.refs_6_
  11.5 0.0 collective-permute-start
  11.5 3.0 %pack.1 = (bf16[136,768]{1,0:T(8,128)(2,1)S(1)}, bf16[136,768]{1,0:T(8,128)(2,1)}, bf16[136,768]{1,0:T(8,128)(2,1)}, bf16[136,768]{1,0:T(8,128)(2,1)}, bf16[136,...) custom-call(s32[1]{0:T(128)} %bitcast.2.me_ref, ...), custom_call_target="tpu_custom_call" | custom-call | tf_op jit(solution)/shard_map/pack/pallas_call | solution.py:380
  14.5 0.0 collective-permute-done.4.refs_5_
  14.5 0.0 collective-permute-done.3.refs_4_
  14.5 0.0 collective-permute-done.2.refs_3_
  14.5 0.0 collective-permute-done.1.refs_2_
  14.6 0.0 collective-permute-done.refs_1_
  14.6 0.6 collective-permute-start.7
  15.2 0.1 collective-permute-start.8
  15.3 1.6 %collective-permute-start.9 = (bf16[136,768]{1,0:T(8,128)(2,1)}, bf16[136,768]{1,0:T(8,128)(2,1)S(1)}, u32[]{:S(2)}, u32[]{:S(2)}) collective-permute-start(bf16[136,768]{1,0:T(8,128)(2,1)} %get-tuple-element.85), channel_id=1, source_target_pairs={{0,3},{1,2},{2,1},{3,0},{4,7},{5,6},{6,5},{7,4},{8,11},{9,10},{10,... | collective-permute-start | bytes 626696 | tf_op jit(solution)/shard_map/ppermute | solution.py:490
  16.9 1.1 collective-permute-start.10
  18.0 2.2 %collective-permute-start.11 = (bf16[136,768]{1,0:T(8,128)(2,1)}, bf16[136,768]{1,0:T(8,128)(2,1)S(1)}, u32[]{:S(2)}, u32[]{:S(2)}) collective-permute-start(bf16[136,768]{1,0:T(8,128)(2,1)} %get-tuple-element.87), channel_id=1, source_target_pairs={{0,5},{1,4},{2,7},{3,6},{4,1},{5,0},{6,3},{7,2},{8,13},{9,12},{10,... | collective-permute-start | bytes 626696 | tf_op jit(solution)/shard_map/ppermute | solution.py:490
  20.2 0.0 collective-permute-done.7.refs_1_
  20.2 1.0 collective-permute-start.12
  21.2 0.9 collective-permute-done.8.refs_2_
  22.1 2.3 %collective-permute-start.13 = (bf16[136,768]{1,0:T(8,128)(2,1)}, bf16[136,768]{1,0:T(8,128)(2,1)S(1)}, u32[]{:S(2)}, u32[]{:S(2)}) collective-permute-start(bf16[136,768]{1,0:T(8,128)(2,1)} %get-tuple-element.89), channel_id=1, source_target_pairs={{0,7},{1,6},{2,5},{3,4},{4,3},{5,2},{6,1},{7,0},{8,15},{9,14},{10,... | collective-permute-start | bytes 626696 | tf_op jit(solution)/shard_map/ppermute | solution.py:490
  24.4 0.0 copy-start
  24.4 0.7 copy-done
  25.0 0.0 copy-start.2
  25.0 0.7 copy-done.2
  25.7 1.8 %index.1 = (f32[24,128]{1,0:T(8,128)S(1)}, f32[1024,128]{1,0:T(8,128)S(1)}, s32[32,128]{1,0:T(8,128)}, s32[1,1]{1,0:T(1,128)}) custom-call(s32[1]{0:T(128)} %bitcast.2.me_ref, s32[8,128]{1,0:T(8,128)S(1)} %bitcast.17, s32[1,128]{1,0:T(1,128)S(1)} %bitcast.25, s32[1,128]{1,0:T(1,128)S(1)} %collective-permute-done.refs_1_, ...), custom_call_target="tpu_custom_call" | custom-call | tf_op jit(solution)/shard_map/index/pallas_call | solution.py:400
  27.5 11.0 %all-to-all-start.1 = ((s32[32,1,128]{2,1,0:T(1,128)}), s32[32,1,128]{2,1,0:T(1,128)S(1)}, u32[]{:S(2)}, u32[]{:S(2)}) async-start(s32[32,1,128]{2,1,0:T(1,128)} %bitcast.6), calls=%async_computation.1 | async-start | bytes 32768 | tf_op jit(solution)/shard_map/all_to_all | solution.py:483
  39.3 7.9 %all-to-all-done.1 = s32[32,1,128]{2,1,0:T(1,128)S(1)} async-done(((s32[32,1,128]{2,1,0:T(1,128)}), s32[32,1,128]{2,1,0:T(1,128)S(1)}, u32[]{:S(2)}, u32[]{:S(2)}) %all-to-all-start.1) | async-done | bytes 16416 | tf_op jit(solution)/shard_map/all_to_all | solution.py:483
  47.2 0.0 collective-permute-done.9.refs_3_
  47.2 0.0 collective-permute-done.10.refs_4_
  47.2 0.0 collective-permute-done.11.refs_5_
  47.2 0.0 collective-permute-done.12.refs_6_
  47.2 0.0 collective-permute-done.13.refs_7_
  47.2 0.1 conditional.1
  47.2 0.1 broadcast.2
  47.3 7.0 %send.1 = bf16[1792,768]{1,0:T(8,128)(2,1)S(1)} custom-call(s32[1]{0:T(128)} %bitcast.2.me_ref, s32[1,1]{1,0:T(1,128)} %get-tuple-element.80.most_ref, s32[32,128]{1,0:T(8,128)S(1)} %bitcast.28, bf16[136,768]{1,0:T(8,128)(2,1)S(1)} %get-tuple-element.82.refs_0_, bf16[136,768]{1,0:T(8,128)(2,1)S(1)} %collective-permute-done.7.refs_1_, ...), custom_call_target="tpu_custom_call" | custom-call | flops 2818572288 | bytes 4000000 | tf_op jit(solution)/shard_map/send/pallas_call | solution.py:417
  54.3 0.0 copy-start.1
  54.3 68.8 %all_to_all.37 = bf16[32,56,768]{2,1,0:T(8,128)(2,1)S(1)} all-to-all(bf16[32,56,768]{2,1,0:T(8,128)(2,1)S(1)} %bitcast.16), channel_id=1, replica_groups=mesh['dp'=32,'seq'=8] {'dp'}, dimensions={0} | all-to-all | bytes 5505024 | tf_op jit(solution)/shard_map/all_to_all | solution.py:483
  123.1 0.0 copy-done.1
  123.1 13.5 %attend.1 = bf16[1024,512]{1,0:T(8,128)(2,1)S(1)} custom-call(s32[1024]{0:T(1024)S(1)} %copy-done.1, s32[1,1]{1,0:T(1,128)} %get-tuple-element.80.most_ref, bf16[1792,768]{1,0:T(8,128)(2,1)S(1)} %bitcast.13, bf16[512,768]{1,0:T(8,128)(2,1)S(1)} %get-tuple-element.92.extra_ref, f32[24,128]{1,0:T(8,128)S(1)} %get-tuple-element.90.rows_ref, ...), custom_call_target="tpu_custom_call" | custom-call | tf_op jit(solution)/shard_map/attend/pallas_call | solution.py:451
  136.6 20.2 %all_to_all.38.returned_ref = bf16[8,128,512]{2,1,0:T(8,128)(2,1)S(1)} all-to-all(bf16[8,128,512]{2,1,0:T(8,128)(2,1)S(1)} %bitcast.14), channel_id=1, replica_groups=mesh['dp'=32,'seq'=8] {'seq'}, dimensions={0} | all-to-all | bytes 2097152 | tf_op jit(solution)/shard_map/all_to_all | solution.py:507
  156.8 1.2 unpack.1
Async XLA Ops:
  0.6 7.8 %collective-permute-start.6 = (s32[1,128]{1,0:T(1,128)}, s32[1,128]{1,0:T(1,128)S(1)}, u32[]{:S(2)}, u32[]{:S(2)}) collective-permute-start(s32[1,128]{1,0:T(1,128)} %bitcast.18), channel_id=1, source_target_pairs={{0,7},{1,6},{2,5},{3,4},{4,3},{5,2},{6,1},{7,0},{8,15},{9,14},{10,... | collective-permute-start | bytes 1544 | tf_op jit(solution)/shard_map/ppermute | solution.py:490
  4.8 6.7 %collective-permute-start.5 = (s32[1,128]{1,0:T(1,128)}, s32[1,128]{1,0:T(1,128)S(1)}, u32[]{:S(2)}, u32[]{:S(2)}) collective-permute-start(s32[1,128]{1,0:T(1,128)} %bitcast.19), channel_id=1, source_target_pairs={{0,6},{1,7},{2,4},{3,5},{4,2},{5,3},{6,0},{7,1},{8,14},{9,15},{10,... | collective-permute-start | bytes 1544 | tf_op jit(solution)/shard_map/ppermute | solution.py:490
  6.5 8.0 %collective-permute-start.4 = (s32[1,128]{1,0:T(1,128)}, s32[1,128]{1,0:T(1,128)S(1)}, u32[]{:S(2)}, u32[]{:S(2)}) collective-permute-start(s32[1,128]{1,0:T(1,128)} %bitcast.20), channel_id=1, source_target_pairs={{0,5},{1,4},{2,7},{3,6},{4,1},{5,0},{6,3},{7,2},{8,13},{9,12},{10,... | collective-permute-start | bytes 1544 | tf_op jit(solution)/shard_map/ppermute | solution.py:490
  6.5 8.0 %collective-permute-start.3 = (s32[1,128]{1,0:T(1,128)}, s32[1,128]{1,0:T(1,128)S(1)}, u32[]{:S(2)}, u32[]{:S(2)}) collective-permute-start(s32[1,128]{1,0:T(1,128)} %bitcast.21), channel_id=1, source_target_pairs={{0,4},{1,5},{2,6},{3,7},{4,0},{5,1},{6,2},{7,3},{8,12},{9,13},{10,... | collective-permute-start | bytes 1544 | tf_op jit(solution)/shard_map/ppermute | solution.py:490
  8.2 6.3 %collective-permute-start.2 = (s32[1,128]{1,0:T(1,128)}, s32[1,128]{1,0:T(1,128)S(1)}, u32[]{:S(2)}, u32[]{:S(2)}) collective-permute-start(s32[1,128]{1,0:T(1,128)} %bitcast.22), channel_id=1, source_target_pairs={{0,3},{1,2},{2,1},{3,0},{4,7},{5,6},{6,5},{7,4},{8,11},{9,10},{10,... | collective-permute-start | bytes 1544 | tf_op jit(solution)/shard_map/ppermute | solution.py:490
  8.5 6.1 %collective-permute-start.1 = (s32[1,128]{1,0:T(1,128)}, s32[1,128]{1,0:T(1,128)S(1)}, u32[]{:S(2)}, u32[]{:S(2)}) collective-permute-start(s32[1,128]{1,0:T(1,128)} %bitcast.23), channel_id=1, source_target_pairs={{0,2},{1,3},{2,0},{3,1},{4,6},{5,7},{6,4},{7,5},{8,10},{9,11},{10,... | collective-permute-start | bytes 1544 | tf_op jit(solution)/shard_map/ppermute | solution.py:490
  11.5 3.0 %collective-permute-start = (s32[1,128]{1,0:T(1,128)}, s32[1,128]{1,0:T(1,128)S(1)}, u32[]{:S(2)}, u32[]{:S(2)}) collective-permute-start(s32[1,128]{1,0:T(1,128)} %bitcast.24), channel_id=1, source_target_pairs={{0,1},{1,0},{2,3},{3,2},{4,5},{5,4},{6,7},{7,6},{8,9},{9,8},{10,11... | collective-permute-start | bytes 1544 | tf_op jit(solution)/shard_map/ppermute | solution.py:490
  14.6 5.6 %collective-permute-start.7 = (bf16[136,768]{1,0:T(8,128)(2,1)}, bf16[136,768]{1,0:T(8,128)(2,1)S(1)}, u32[]{:S(2)}, u32[]{:S(2)}) collective-permute-start(bf16[136,768]{1,0:T(8,128)(2,1)} %get-tuple-element.83), channel_id=1, source_target_pairs={{0,1},{1,0},{2,3},{3,2},{4,5},{5,4},{6,7},{7,6},{8,9},{9,8},{10,11... | collective-permute-start | bytes 626696 | tf_op jit(solution)/shard_map/ppermute | solution.py:490
  15.2 6.9 %collective-permute-start.8 = (bf16[136,768]{1,0:T(8,128)(2,1)}, bf16[136,768]{1,0:T(8,128)(2,1)S(1)}, u32[]{:S(2)}, u32[]{:S(2)}) collective-permute-start(bf16[136,768]{1,0:T(8,128)(2,1)} %get-tuple-element.84), channel_id=1, source_target_pairs={{0,2},{1,3},{2,0},{3,1},{4,6},{5,7},{6,4},{7,5},{8,10},{9,11},{10,... | collective-permute-start | bytes 626696 | tf_op jit(solution)/shard_map/ppermute | solution.py:490
  15.3 31.9 %collective-permute-start.9 = (bf16[136,768]{1,0:T(8,128)(2,1)}, bf16[136,768]{1,0:T(8,128)(2,1)S(1)}, u32[]{:S(2)}, u32[]{:S(2)}) collective-permute-start(bf16[136,768]{1,0:T(8,128)(2,1)} %get-tuple-element.85), channel_id=1, source_target_pairs={{0,3},{1,2},{2,1},{3,0},{4,7},{5,6},{6,5},{7,4},{8,11},{9,10},{10,... | collective-permute-start | bytes 626696 | tf_op jit(solution)/shard_map/ppermute | solution.py:490
  16.9 30.3 %collective-permute-start.10 = (bf16[136,768]{1,0:T(8,128)(2,1)}, bf16[136,768]{1,0:T(8,128)(2,1)S(1)}, u32[]{:S(2)}, u32[]{:S(2)}) collective-permute-start(bf16[136,768]{1,0:T(8,128)(2,1)} %get-tuple-element.86), channel_id=1, source_target_pairs={{0,4},{1,5},{2,6},{3,7},{4,0},{5,1},{6,2},{7,3},{8,12},{9,13},{10,... | collective-permute-start | bytes 626696 | tf_op jit(solution)/shard_map/ppermute | solution.py:490
  18.0 29.2 %collective-permute-start.11 = (bf16[136,768]{1,0:T(8,128)(2,1)}, bf16[136,768]{1,0:T(8,128)(2,1)S(1)}, u32[]{:S(2)}, u32[]{:S(2)}) collective-permute-start(bf16[136,768]{1,0:T(8,128)(2,1)} %get-tuple-element.87), channel_id=1, source_target_pairs={{0,5},{1,4},{2,7},{3,6},{4,1},{5,0},{6,3},{7,2},{8,13},{9,12},{10,... | collective-permute-start | bytes 626696 | tf_op jit(solution)/shard_map/ppermute | solution.py:490
  20.2 27.0 %collective-permute-start.12 = (bf16[136,768]{1,0:T(8,128)(2,1)}, bf16[136,768]{1,0:T(8,128)(2,1)S(1)}, u32[]{:S(2)}, u32[]{:S(2)}) collective-permute-start(bf16[136,768]{1,0:T(8,128)(2,1)} %get-tuple-element.88), channel_id=1, source_target_pairs={{0,6},{1,7},{2,4},{3,5},{4,2},{5,3},{6,0},{7,1},{8,14},{9,15},{10,... | collective-permute-start | bytes 626696 | tf_op jit(solution)/shard_map/ppermute | solution.py:490
  22.1 25.1 %collective-permute-start.13 = (bf16[136,768]{1,0:T(8,128)(2,1)}, bf16[136,768]{1,0:T(8,128)(2,1)S(1)}, u32[]{:S(2)}, u32[]{:S(2)}) collective-permute-start(bf16[136,768]{1,0:T(8,128)(2,1)} %get-tuple-element.89), channel_id=1, source_target_pairs={{0,7},{1,6},{2,5},{3,4},{4,3},{5,2},{6,1},{7,0},{8,15},{9,14},{10,... | collective-permute-start | bytes 626696 | tf_op jit(solution)/shard_map/ppermute | solution.py:490
  24.4 0.7 copy-start
  25.0 0.7 copy-start.2
  27.5 19.7 %all-to-all-start.1 = ((s32[32,1,128]{2,1,0:T(1,128)}), s32[32,1,128]{2,1,0:T(1,128)S(1)}, u32[]{:S(2)}, u32[]{:S(2)}) async-start(s32[32,1,128]{2,1,0:T(1,128)} %bitcast.6), calls=%async_computation.1 | async-start | bytes 32768 | tf_op jit(solution)/shard_map/all_to_all | solution.py:483
  54.3 68.8 %copy-start.1 = (s32[1024]{0:T(1024)S(1)}, s32[1024]{0:T(1024)}, u32[]{:S(2)}) copy-start(s32[1024]{0:T(1024)} %segment_ref.1) | copy-start | bytes 12292

commit v2 on v0

--- a/solution.py
+++ b/solution.py
@@ -9,6 +9,8 @@
 
 HEAD_DIM = 128
 N_DP = 32
+N_Z = 8
+N_X = 4
 N_SEQ = 8
 ROWS = 128
 GROUP = N_SEQ * ROWS
@@ -90,7 +92,10 @@
     return jnp.concatenate([rows[s : s + 1] for s in range(N_SEQ)], axis=1)
 
 
-def index_kernel(list_ref, segment_ref, rows_ref, cols_ref, request_ref, most_ref):
+def index_kernel(me_ref, segment_ref, *refs):
+    lists, (rows_ref, cols_ref, request_ref, most_ref, list_ref) = refs[:N_SEQ], refs[N_SEQ:]
+    for m in range(N_SEQ):
+        list_ref[pl.ds(jnp.bitwise_xor(me_ref[0], m), 1), :] = lists[m][...]
     listed = list_ref[...]
     source = (listed // GROUP).astype(jnp.float32)
     local_row = (listed % ROWS).astype(jnp.float32)
@@ -129,27 +134,26 @@
     most_ref[0, 0] = (jnp.max(slot) + 1.0).astype(jnp.int32)
 
 
-def request_picks(turned, group, first, capacity, width):
+def turned_requests(request_ref):
+    blank = jnp.zeros((LANES - N_DP, LANES), jnp.float32)
+    return jnp.concatenate([request_ref[...].astype(jnp.float32), blank], axis=0).T - 1.0
+
+
+def group_picks(turned, group, first, capacity):
     column = jnp.concatenate(
         [turned[first : first + capacity, d : d + 1] for d in range(8 * group, 8 * group + 8)], axis=0
     )
-    row_id = iota((8 * capacity, width), 1).astype(jnp.float32)
+    row_id = iota((8 * capacity, GROUP), 1).astype(jnp.float32)
     return (column == row_id).astype(jnp.float32).astype(jnp.bfloat16)
-
-
-def turned_requests(request_ref):
-    blank = jnp.zeros((LANES - N_DP, LANES), jnp.float32)
-    turned = jnp.concatenate([request_ref[...].astype(jnp.float32), blank], axis=0).T
-    delta_id = (iota((LANES, LANES), 1) + GROUP).astype(jnp.float32)
-    return jnp.where(iota((LANES, LANES), 0) == 0, delta_id, turned - 1.0)
 
 
 def join_columns(me_ref, parts, ext_ref, delta_ref):
     for m in range(N_SEQ):
         column = jnp.bitwise_xor(me_ref[0], m)
-        ext_ref[pl.ds(pl.multiple_of(column * ROWS, ROWS), ROWS), :] = parts[m][:ROWS, :]
+        whole = parts[m][...]
+        ext_ref[pl.ds(pl.multiple_of(column * ROWS, ROWS), ROWS), :] = whole[:ROWS]
         if delta_ref is not None:
-            delta_ref[column] = parts[m][ROWS:, :LANES].astype(jnp.float32)
+            delta_ref[column] = whole[ROWS:, :LANES].astype(jnp.float32)
 
 
 def send_extra_kernel(me_ref, request_ref, *refs):
@@ -158,13 +162,13 @@
     turned = turned_requests(request_ref)
     join_columns(me_ref, parts, ext_ref, None)
     for group in range(N_DP // 8):
-        pick = request_picks(turned, group, CAPACITY, EXTRA, GROUP)
+        pick = group_picks(turned, group, CAPACITY, EXTRA)
         rows = slice(group * group_rows, (group + 1) * group_rows)
         sent_ref[rows, :] = nn_dot(pick, ext_ref[...]).astype(jnp.bfloat16)
 
 
 def send_kernel(me_ref, most_ref, request_ref, *refs):
-    parts, (sent_ref, pick_ref, ext_ref, place_ref, delta_ref) = refs[:N_SEQ], refs[N_SEQ:]
+    parts, (sent_ref, ext_ref, place_ref, delta_ref) = refs[:N_SEQ], refs[N_SEQ:]
     capacity = CAPACITY
     group_rows = 8 * capacity
     turned = turned_requests(request_ref)
@@ -177,21 +181,21 @@
         value = jnp.where(
             iota((8, 8 * count), 0) == 0, owner + 8 * group, index - owner * count + first
         )
-        return nn_dot(value.astype(jnp.float32).astype(jnp.bfloat16), pick[:, :GROUP])
+        return nn_dot(value.astype(jnp.float32).astype(jnp.bfloat16), pick)
 
     place = jnp.zeros((8, GROUP), jnp.float32)
     for group in range(N_DP // 8):
-        pick = request_picks(turned, group, 0, capacity, GROUP + LANES)
-        pick_ref[group * group_rows : (group + 1) * group_rows, :] = pick
+        pick = group_picks(turned, group, 0, capacity)
         place = place + places(pick, group, 0, capacity)
+        rows = slice(group * group_rows, (group + 1) * group_rows)
+        sent_ref[rows, :] = nn_dot(pick, ext_ref[...]).astype(jnp.bfloat16)
     place_ref[...] = place
 
     @pl.when(most_ref[0, 0] >= CAPACITY)
     def _():
         more = jnp.zeros((8, GROUP), jnp.float32)
         for group in range(N_DP // 8):
-            pick = request_picks(turned, group, CAPACITY, EXTRA, GROUP)
-            more = more + places(pick, group, CAPACITY, EXTRA)
+            more = more + places(group_picks(turned, group, CAPACITY, EXTRA), group, CAPACITY, EXTRA)
         place_ref[...] += more
 
     place = place_ref[...]
@@ -211,19 +215,19 @@
         )
         slot_pick = (slot_col + (64.0 * head - 1.0) == lane).astype(jnp.float32)
         tail = tail + nn_dot(spread.astype(jnp.bfloat16), slot_pick.astype(jnp.bfloat16))
-    tail = jnp.concatenate(
-        [tail[:N_DP], tail[N_DP:], jnp.zeros((N_DP, WIDTH - 2 * LANES), jnp.float32)], axis=1
-    )
-    tail = jnp.concatenate([tail, jnp.zeros((LANES - N_DP, WIDTH), jnp.float32)], axis=0)
-    ext_ref[GROUP:, :] = tail.astype(jnp.bfloat16)
-    for group in range(N_DP // 8):
-        rows = slice(group * group_rows, (group + 1) * group_rows)
-        sent_ref[rows, :] = nn_dot(pick_ref[rows, :], ext_ref[...]).astype(jnp.bfloat16)
+    tail = jnp.concatenate([tail[:N_DP], tail[N_DP:]], axis=1)
+    row = iota((16, 2 * LANES), 0)
+    for owner in range(N_DP):
+        inside = owner * capacity % 16
+        rows = slice(owner * capacity - inside, owner * capacity - inside + 16)
+        kept = sent_ref[rows, : 2 * LANES].astype(jnp.float32)
+        mine = jnp.broadcast_to(tail[owner : owner + 1], (16, 2 * LANES))
+        sent_ref[rows, : 2 * LANES] = jnp.where(row == inside, mine, kept).astype(jnp.bfloat16)
 
 
 def attend_kernel(
     segment_ref, most_ref, arrived_ref, extra_ref, rows_ref, cols_ref, out_ref,
-    x_ref, kt_ref, delta_ref, weight_ref, squash_ref, total_ref, gqt_ref, gk_ref, gv_ref,
+    x_ref, kt_ref, lanes_ref, weight_ref, squash_ref, total_ref, gqt_ref, gk_ref, gv_ref,
 ):
     slots = N_DP * CAPACITY
     blocks = GROUP // BLOCK
@@ -261,57 +265,72 @@
     both = nn_dot(high, from_source) + nn_dot(low, from_source)
     place = iota((LANES, GROUP), 0).astype(jnp.float32)
     for head in range(2):
-        delta_ref[head : head + 1, :] = jnp.sum(
+        lanes_ref[head : head + 1, :] = jnp.sum(
             jnp.where(place == slot + 64.0 * head, both, 0.0), axis=0, keepdims=True
         )
     gk_ref[...] = jnp.zeros_like(gk_ref)
     gv_ref[...] = jnp.zeros_like(gv_ref)
-    causal = iota((BLOCK, BLOCK), 0) <= iota((BLOCK, BLOCK), 1)
-    causal = jnp.concatenate([causal.astype(jnp.float32)] * 2, axis=1) > 0.0
+
     for block in range(blocks):
         rows = slice(block * BLOCK, (block + 1) * BLOCK)
+        near = slice(max(block - 1, 0) * BLOCK, (block + 1) * BLOCK)
+        near_count = near.stop - near.start
         queries = jnp.concatenate([x_ref[rows, 0:128], x_ref[rows, 128:256]], axis=0)
         grads = jnp.concatenate([x_ref[rows, 512:640], x_ref[rows, 640:768]], axis=0)
-        delta = jnp.concatenate([delta_ref[0:1, rows], delta_ref[1:2, rows]], axis=1)
+        delta = jnp.concatenate([lanes_ref[0:1, rows], lanes_ref[1:2, rows]], axis=1)
         segment_q = jnp.concatenate([segment[:, rows]] * 2, axis=1)
-
-        def weigh(key_block):
-            keys = slice(key_block * BLOCK, (key_block + 1) * BLOCK)
+        far = range(block - 1)
+
+        def weigh(keys, causal):
             score = nt_dot(x_ref[keys, 256:384], queries)
             squashed = jnp.tanh(score * (scaling / softcap))
             allowed = cols_ref[keys, 2:3] == segment_q
-            if key_block == block:
+            if causal is not None:
                 allowed = allowed & causal
-            weights = jnp.where(allowed, jnp.exp(softcap * squashed), 0.0)
-            weight_ref[keys, :] = weights
-            squash_ref[keys, :] = squashed
-            total = jnp.sum(weights, axis=0, keepdims=True)
-            if key_block == block:
-                total_ref[0:1, :] = total
-            else:
-                total_ref[0:1, :] += total
-
-        def back(key_block):
-            keys = slice(key_block * BLOCK, (key_block + 1) * BLOCK)
-            probabilities = weight_ref[keys, :] * (1.0 / total_ref[0:1, :])
+            return squashed, jnp.where(allowed, jnp.exp(softcap * squashed), 0.0)
+
+        def back(keys, squashed, weights, inverse):
+            probabilities = weights * inverse
             gv_ref[keys, :] += nn_dot(probabilities.astype(jnp.bfloat16), grads)
             prob_grad = nt_dot(x_ref[keys, 384:512], grads)
-            squashed = squash_ref[keys, :]
             score_grad = probabilities * (prob_grad - delta) * (1.0 - squashed * squashed)
             score_grad = score_grad.astype(jnp.bfloat16)
             gk_ref[keys, :] += nn_dot(score_grad, queries)
-            part = nn_dot(kt_ref[:, keys], score_grad)
-            if key_block == block:
-                gqt_ref[...] = part
-            else:
-                gqt_ref[...] += part
-
-        first_segment = segment_ref[block * BLOCK]
-        for step in (weigh, back):
-            step(block)
-            for key_block in range(block):
-                meets = segment_ref[(key_block + 1) * BLOCK - 1] == first_segment
-                pl.when(meets)(functools.partial(step, key_block))
+            return nn_dot(kt_ref[:, keys], score_grad)
+
+        def reaches(key_block):
+            return segment_ref[(key_block + 1) * BLOCK - 1] == segment_ref[block * BLOCK]
+
+        if len(far) > 0:
+            total_ref[...] = jnp.zeros_like(total_ref)
+        for key_block in far:
+
+            @pl.when(reaches(key_block))
+            def _(keys=slice(key_block * BLOCK, (key_block + 1) * BLOCK)):
+                squashed, weights = weigh(keys, None)
+                weight_ref[keys, :] = weights
+                squash_ref[keys, :] = squashed
+                total_ref[0:1, :] += jnp.sum(weights, axis=0, keepdims=True)
+
+        ahead = iota((near_count, BLOCK), 0) - iota((near_count, BLOCK), 1)
+        causal = (ahead <= near_count - BLOCK).astype(jnp.float32)
+        causal = jnp.concatenate([causal, causal], axis=1) > 0.0
+        squashed, weights = weigh(near, causal)
+        total = jnp.sum(weights, axis=0, keepdims=True)
+        if len(far) > 0:
+            total = total + total_ref[0:1, :]
+        inverse = 1.0 / total
+        gqt_ref[...] = back(near, squashed, weights, inverse)
+        if len(far) > 0:
+            total_ref[0:1, :] = inverse
+        for key_block in far:
+
+            @pl.when(reaches(key_block))
+            def _(keys=slice(key_block * BLOCK, (key_block + 1) * BLOCK)):
+                gqt_ref[...] += back(
+                    keys, squash_ref[keys, :], weight_ref[keys, :], total_ref[0:1, :]
+                )
+
         turned = (gqt_ref[...].T * scaling).astype(jnp.bfloat16)
         out_ref[rows, 0:128] = turned[:BLOCK]
         out_ref[rows, 128:256] = turned[BLOCK:]
@@ -360,8 +379,7 @@
     )(me, query, key_rows, value_rows, attn_out, out_grad)
 
 
-def index(pack_list, segments):
-    vmem = pl.BlockSpec(memory_space=pltpu.VMEM)
+def index(me, segments, lists):
     return pl.pallas_call(
         index_kernel,
         out_shape=(
@@ -370,10 +388,12 @@
             shape((N_DP, LANES), jnp.int32),
             shape((1, 1), jnp.int32),
         ),
-        out_specs=(vmem, vmem, vmem, pl.BlockSpec(memory_space=pltpu.SMEM)),
+        in_specs=[SMEM] + [VMEM] * 9,
+        out_specs=(VMEM, VMEM, VMEM, SMEM),
+        scratch_shapes=[pltpu.VMEM((N_SEQ, LANES), jnp.int32)],
         compiler_params=PARAMS,
         name="index",
-    )(pack_list, segments.reshape(N_SEQ, ROWS))
+    )(me, segments.reshape(N_SEQ, ROWS), *lists)
 
 
 def send(me, most, request, parts):
@@ -382,8 +402,7 @@
         out_shape=shape((N_DP * CAPACITY, WIDTH)),
         in_specs=[SMEM, SMEM] + [VMEM] * 9,
         scratch_shapes=[
-            pltpu.VMEM((N_DP * CAPACITY, GROUP + LANES), jnp.bfloat16),
-            pltpu.VMEM((GROUP + LANES, WIDTH), jnp.bfloat16),
+            pltpu.VMEM((GROUP, WIDTH), jnp.bfloat16),
             pltpu.VMEM((8, GROUP), jnp.float32),
             pltpu.VMEM((N_SEQ, 8, LANES), jnp.float32),
         ],
@@ -413,8 +432,8 @@
             pltpu.VMEM((GROUP, WIDTH), jnp.bfloat16),
             pltpu.VMEM((HEAD_DIM, GROUP), jnp.bfloat16),
             pltpu.VMEM((8, GROUP), jnp.float32),
-            pltpu.VMEM((GROUP, 2 * BLOCK), jnp.float32),
-            pltpu.VMEM((GROUP, 2 * BLOCK), jnp.float32),
+            pltpu.VMEM((GROUP - 2 * BLOCK, 2 * BLOCK), jnp.float32),
+            pltpu.VMEM((GROUP - 2 * BLOCK, 2 * BLOCK), jnp.float32),
             pltpu.VMEM((8, 2 * BLOCK), jnp.float32),
             pltpu.VMEM((HEAD_DIM, 2 * BLOCK), jnp.float32),
             pltpu.VMEM((GROUP, HEAD_DIM), jnp.float32),
@@ -438,16 +457,28 @@
     return lax.all_to_all(array, "dp", split_axis=0, concat_axis=0, tiled=True)
 
 
+def relay_requests(request):
+    along_x = [[z * N_X + x for x in range(N_X)] for z in range(N_Z)]
+    along_z = [[z * N_X + x for z in range(N_Z)] for x in range(N_X)]
+    request = request.reshape(N_Z, N_X, LANES).transpose(1, 0, 2)
+    request = lax.all_to_all(request, "dp", 0, 0, axis_index_groups=along_x, tiled=True)
+    request = request.transpose(1, 0, 2)
+    request = lax.all_to_all(request, "dp", 0, 0, axis_index_groups=along_z, tiled=True)
+    return request.reshape(N_DP, LANES)
+
+
 def local(query, key_rows, value_rows, attn_out, out_grad, source_row, segment_ids):
     me = lax.axis_index("seq").reshape(1)
+
+    def swap(array, m):
+        return lax.ppermute(array, "seq", [(s, s ^ m) for s in range(N_SEQ)]) if m else array
+
+    lists = [swap(source_row.reshape(1, ROWS), m) for m in range(N_SEQ)]
     packed = pack(me, query, key_rows, value_rows, attn_out, out_grad)
-    packed, source_row = lax.optimization_barrier((packed, source_row))
-    parts = [packed[0]]
-    for m in range(1, N_SEQ):
-        parts.append(lax.ppermute(packed[m], "seq", [(s, s ^ m) for s in range(N_SEQ)]))
-    pack_list = lax.all_gather(source_row, "seq", axis=0)
-    rows, cols, request, most = index(pack_list, segment_ids)
-    request = relay(request)
+    packed, lists = lax.optimization_barrier((packed, lists))
+    parts = [swap(packed[m], m) for m in range(N_SEQ)]
+    rows, cols, request, most = index(me, segment_ids, lists)
+    request = relay_requests(request)
     arrived = relay(send(me, most, request, parts))
     extra = lax.cond(
         most[0, 0] >= CAPACITY,

time: 165 us -> 155 us (0.939)
  blocking collectives: 108 us -> 94.8 us
  starting transfers between devices: 22.6 us -> 28 us
  waiting for transfers between devices: 8.78 us -> 6.88 us
    all_gather x1 -> x0, blocking collectives: 21.7 us -> none  [local(): pack_list = lax.all_gather(source_row, 'seq', axis=0)]
    all_to_all x0 -> x1, blocking collectives: none -> 8.32 us  [relay_requests(): lax.all_to_all(request, 'dp', 0, 0, axis_index_groups=along_x, tiled=True)]
    ppermute x7 -> x14, starting transfers between devices: 11.6 us -> 19.8 us  [swap(): lax.ppermute(array, 'seq', [(s, s ^ m) for s in range(N_SEQ)])]
    all_to_all x1, starting transfers between devices: 11 us -> 8.19 us  [relay_requests(): lax.all_to_all(request, 'dp', 0, 0, axis_index_groups=along_z, tiled=True)]
    all_to_all x1, waiting for transfers between devices: 7.86 us -> 5.97 us  [relay_requests(): lax.all_to_all(request, 'dp', 0, 0, axis_index_groups=along_z, tiled=True)]
  transfers between devices with their start and end apart: 8 -> 15, of which waited for: 2 -> 2; matrix products, arithmetic and copies ran while one was open for 0% -> 0% of each run, Pallas kernels for 1% -> 3%
where the time goes in v2:
time: 155 us
  blocking collectives  94.8 us (61%)
  starting transfers between devices  28 us (18%)
  Pallas kernels  21.5 us (14%)
  waiting for transfers between devices  6.88 us (4%)
  local copies, waits for them, and re-layouts  2.02 us (1%)
    all_to_all x1, blocking collectives, relay(): return lax.all_to_all(array, 'dp', split_axis=0, concat_axis=0, tiled=True)  65.9 us
    all_to_all x1, blocking collectives, local(): lax.all_to_all(grads.reshape(N_SEQ, ROWS, 4 * HEAD_DIM), 'seq', split_axi...  20.6 us
    ppermute x14, starting transfers between devices, swap(): lax.ppermute(array, 'seq', [(s, s ^ m) for s in range(N_SEQ)])  19.8 us
    pallas_call x1, Pallas kernels, attend(): pl.pallas_call(attend_kernel, out_shape=shape((GROUP, 4 * HEAD_DIM)), in_...  10.5 us
    all_to_all x1, blocking collectives, relay_requests(): lax.all_to_all(request, 'dp', 0, 0, axis_index_groups=along_x, tiled=True)  8.32 us
    all_to_all x1, starting transfers between devices, relay_requests(): lax.all_to_all(request, 'dp', 0, 0, axis_index_groups=along_z, tiled=True)  8.19 us
    all_to_all x1, waiting for transfers between devices, relay_requests(): lax.all_to_all(request, 'dp', 0, 0, axis_index_groups=along_z, tiled=True)  5.97 us
    pallas_call x1, Pallas kernels, send(): pl.pallas_call(send_kernel, out_shape=shape((N_DP * CAPACITY, WIDTH)), in...  5.17 us
  transfers between devices with their start and end apart: 15, of which 2 were waited for; matrix products, arithmetic and copies ran while one was open for 0% of the time, Pallas kernels for 3%

profile of v2, /device:TPU:1, one launch (start us, length us, event | category | flops | bytes accessed | tf_op | source)
XLA Modules:
  0.0 154.8 jit_solution(14563929823520297863)
XLA Ops:
  0.6 4.2 %collective-permute-start.6 = (s32[1,128]{1,0:T(1,128)}, s32[1,128]{1,0:T(1,128)S(1)}, u32[]{:S(2)}, u32[]{:S(2)}) collective-permute-start(s32[1,128]{1,0:T(1,128)} %bitcast.21), channel_id=1, source_target_pairs={{0,7},{1,6},{2,5},{3,4},{4,3},{5,2},{6,1},{7,0},{8,15},{9,14},{10,... | collective-permute-start | bytes 1544 | tf_op jit(solution)/shard_map/ppermute | solution.py:474
  4.8 1.7 %collective-permute-start.5 = (s32[1,128]{1,0:T(1,128)}, s32[1,128]{1,0:T(1,128)S(1)}, u32[]{:S(2)}, u32[]{:S(2)}) collective-permute-start(s32[1,128]{1,0:T(1,128)} %bitcast.22), channel_id=1, source_target_pairs={{0,6},{1,7},{2,4},{3,5},{4,2},{5,3},{6,0},{7,1},{8,14},{9,15},{10,... | collective-permute-start | bytes 1544 | tf_op jit(solution)/shard_map/ppermute | solution.py:474
  6.5 0.0 collective-permute-start.4
  6.5 1.7 %collective-permute-start.3 = (s32[1,128]{1,0:T(1,128)}, s32[1,128]{1,0:T(1,128)S(1)}, u32[]{:S(2)}, u32[]{:S(2)}) collective-permute-start(s32[1,128]{1,0:T(1,128)} %bitcast.24), channel_id=1, source_target_pairs={{0,4},{1,5},{2,6},{3,7},{4,0},{5,1},{6,2},{7,3},{8,12},{9,13},{10,... | collective-permute-start | bytes 1544 | tf_op jit(solution)/shard_map/ppermute | solution.py:474
  8.2 0.3 collective-permute-start.2
  8.4 0.0 collective-permute-done.6.refs_7_
  8.5 3.1 %collective-permute-start.1 = (s32[1,128]{1,0:T(1,128)}, s32[1,128]{1,0:T(1,128)S(1)}, u32[]{:S(2)}, u32[]{:S(2)}) collective-permute-start(s32[1,128]{1,0:T(1,128)} %bitcast.26), channel_id=1, source_target_pairs={{0,2},{1,3},{2,0},{3,1},{4,6},{5,7},{6,4},{7,5},{8,10},{9,11},{10,... | collective-permute-start | bytes 1544 | tf_op jit(solution)/shard_map/ppermute | solution.py:474
  11.5 0.0 collective-permute-done.5.refs_6_
  11.5 0.0 collective-permute-start
  11.5 3.0 %pack.1 = (bf16[136,768]{1,0:T(8,128)(2,1)S(1)}, bf16[136,768]{1,0:T(8,128)(2,1)}, bf16[136,768]{1,0:T(8,128)(2,1)}, bf16[136,768]{1,0:T(8,128)(2,1)}, bf16[136,...) custom-call(s32[1]{0:T(128)} %bitcast.2.me_ref, ...), custom_call_target="tpu_custom_call" | custom-call | tf_op jit(solution)/shard_map/pack/pallas_call | solution.py:363
  14.5 0.0 collective-permute-done.4.refs_5_
  14.5 0.0 collective-permute-done.3.refs_4_
  14.5 0.0 collective-permute-done.2.refs_3_
  14.5 0.0 collective-permute-done.1.refs_2_
  14.6 0.0 collective-permute-done.refs_1_
  14.6 0.6 collective-permute-start.7
  15.2 0.1 collective-permute-start.8
  15.3 1.6 %collective-permute-start.9 = (bf16[136,768]{1,0:T(8,128)(2,1)}, bf16[136,768]{1,0:T(8,128)(2,1)S(1)}, u32[]{:S(2)}, u32[]{:S(2)}) collective-permute-start(bf16[136,768]{1,0:T(8,128)(2,1)} %get-tuple-element.85), channel_id=1, source_target_pairs={{0,3},{1,2},{2,1},{3,0},{4,7},{5,6},{6,5},{7,4},{8,11},{9,10},{10,... | collective-permute-start | bytes 626696 | tf_op jit(solution)/shard_map/ppermute | solution.py:474
  16.9 1.1 collective-permute-start.10
  18.0 2.2 %collective-permute-start.11 = (bf16[136,768]{1,0:T(8,128)(2,1)}, bf16[136,768]{1,0:T(8,128)(2,1)S(1)}, u32[]{:S(2)}, u32[]{:S(2)}) collective-permute-start(bf16[136,768]{1,0:T(8,128)(2,1)} %get-tuple-element.87), channel_id=1, source_target_pairs={{0,5},{1,4},{2,7},{3,6},{4,1},{5,0},{6,3},{7,2},{8,13},{9,12},{10,... | collective-permute-start | bytes 626696 | tf_op jit(solution)/shard_map/ppermute | solution.py:474
  20.2 0.0 collective-permute-done.7.refs_1_
  20.2 1.0 collective-permute-start.12
  21.2 0.9 collective-permute-done.8.refs_2_
  22.1 2.3 %collective-permute-start.13 = (bf16[136,768]{1,0:T(8,128)(2,1)}, bf16[136,768]{1,0:T(8,128)(2,1)S(1)}, u32[]{:S(2)}, u32[]{:S(2)}) collective-permute-start(bf16[136,768]{1,0:T(8,128)(2,1)} %get-tuple-element.89), channel_id=1, source_target_pairs={{0,7},{1,6},{2,5},{3,4},{4,3},{5,2},{6,1},{7,0},{8,15},{9,14},{10,... | collective-permute-start | bytes 626696 | tf_op jit(solution)/shard_map/ppermute | solution.py:474
  24.4 0.0 copy-start
  24.4 0.7 copy-done
  25.0 0.0 copy-start.2
  25.0 0.7 copy-done.2
  25.7 1.7 %index.1 = (f32[24,128]{1,0:T(8,128)S(1)}, f32[1024,128]{1,0:T(8,128)S(1)}, s32[32,128]{1,0:T(8,128)S(1)}, s32[1,1]{1,0:T(1,128)}) custom-call(s32[1]{0:T(128)} %bitcast.2.me_ref, s32[8,128]{1,0:T(8,128)S(1)} %bitcast.20, s32[1,128]{1,0:T(1,128)S(1)} %bitcast.28, s32[1,128]{1,0:T(1,128)S(1)} %collective-permute-done.refs_1_, ...), custom_call_target="tpu_custom_call" | custom-call | tf_op jit(solution)/shard_map/index/pallas_call | solution.py:383
  27.4 8.3 %all_to_all.36 = s32[4,8,128]{2,1,0:T(8,128)S(1)} all-to-all(s32[4,8,128]{2,1,0:T(8,128)S(1)} %bitcast.32), channel_id=1, replica_groups={{0,8,16,24},{32,40,48,56},{64,72,80,88},{96,104,112,120},{128,136,144,1..., dimensions={0} | all-to-all | bytes 32768 | tf_op jit(solution)/shard_map/all_to_all | solution.py:464
  35.7 0.6 copy.13
  36.3 8.2 %all-to-all-start.2 = ((s32[8,4,128]{2,1,0:T(4,128)}), s32[8,4,128]{2,1,0:T(4,128)S(1)}, u32[]{:S(2)}, u32[]{:S(2)}) async-start(s32[8,4,128]{2,1,0:T(4,128)} %copy.13), calls=%async_computation.2 | async-start | bytes 32768 | tf_op jit(solution)/shard_map/all_to_all | solution.py:466
  45.2 6.0 %all-to-all-done.2 = s32[8,4,128]{2,1,0:T(4,128)S(1)} async-done(((s32[8,4,128]{2,1,0:T(4,128)}), s32[8,4,128]{2,1,0:T(4,128)S(1)}, u32[]{:S(2)}, u32[]{:S(2)}) %all-to-all-start.2) | async-done | bytes 16416 | tf_op jit(solution)/shard_map/all_to_all | solution.py:466
  51.1 0.0 collective-permute-done.9.refs_3_
  51.2 0.0 collective-permute-done.10.refs_4_
  51.2 0.0 collective-permute-done.11.refs_5_
  51.2 0.0 collective-permute-done.12.refs_6_
  51.2 0.0 collective-permute-done.13.refs_7_
  51.2 0.3 conditional.1
  51.2 0.1 broadcast.2
  51.4 5.2 %send.1 = bf16[1792,768]{1,0:T(8,128)(2,1)S(1)} custom-call(s32[1]{0:T(128)} %bitcast.2.me_ref, s32[1,1]{1,0:T(1,128)} %get-tuple-element.80.most_ref, s32[32,128]{1,0:T(8,128)S(1)} %bitcast.31, bf16[136,768]{1,0:T(8,128)(2,1)S(1)} %get-tuple-element.82.refs_0_, bf16[136,768]{1,0:T(8,128)(2,1)S(1)} %collective-permute-done.7.refs_1_, ...), custom_call_target="tpu_custom_call" | custom-call | flops 2818572288 | bytes 4000000 | tf_op jit(solution)/shard_map/send/pallas_call | solution.py:400
  56.6 0.0 copy-start.1
  56.6 65.9 %all_to_all.37 = bf16[32,56,768]{2,1,0:T(8,128)(2,1)S(1)} all-to-all(bf16[32,56,768]{2,1,0:T(8,128)(2,1)S(1)} %bitcast.18), channel_id=1, replica_groups=mesh['dp'=32,'seq'=8] {'dp'}, dimensions={0} | all-to-all | bytes 5505024 | tf_op jit(solution)/shard_map/all_to_all | solution.py:457
  122.5 0.0 copy-done.1
  122.5 10.5 %attend.1 = bf16[1024,512]{1,0:T(8,128)(2,1)S(1)} custom-call(s32[1024]{0:T(1024)S(1)} %copy-done.1, s32[1,1]{1,0:T(1,128)} %get-tuple-element.80.most_ref, bf16[1792,768]{1,0:T(8,128)(2,1)S(1)} %bitcast.15, bf16[512,768]{1,0:T(8,128)(2,1)S(1)} %get-tuple-element.92.extra_ref, f32[24,128]{1,0:T(8,128)S(1)} %get-tuple-element.90.rows_ref, ...), custom_call_target="tpu_custom_call" | custom-call | tf_op jit(solution)/shard_map/attend/pallas_call | solution.py:427
  133.0 20.6 %all_to_all.38.returned_ref = bf16[8,128,512]{2,1,0:T(8,128)(2,1)S(1)} all-to-all(bf16[8,128,512]{2,1,0:T(8,128)(2,1)S(1)} %bitcast.16), channel_id=1, replica_groups=mesh['dp'=32,'seq'=8] {'seq'}, dimensions={0} | all-to-all | bytes 2097152 | tf_op jit(solution)/shard_map/all_to_all | solution.py:491
  153.6 1.2 unpack.1
  (1 shorter events, 0.0 us)
Async XLA Ops:
  0.6 7.8 %collective-permute-start.6 = (s32[1,128]{1,0:T(1,128)}, s32[1,128]{1,0:T(1,128)S(1)}, u32[]{:S(2)}, u32[]{:S(2)}) collective-permute-start(s32[1,128]{1,0:T(1,128)} %bitcast.21), channel_id=1, source_target_pairs={{0,7},{1,6},{2,5},{3,4},{4,3},{5,2},{6,1},{7,0},{8,15},{9,14},{10,... | collective-permute-start | bytes 1544 | tf_op jit(solution)/shard_map/ppermute | solution.py:474
  4.8 6.7 %collective-permute-start.5 = (s32[1,128]{1,0:T(1,128)}, s32[1,128]{1,0:T(1,128)S(1)}, u32[]{:S(2)}, u32[]{:S(2)}) collective-permute-start(s32[1,128]{1,0:T(1,128)} %bitcast.22), channel_id=1, source_target_pairs={{0,6},{1,7},{2,4},{3,5},{4,2},{5,3},{6,0},{7,1},{8,14},{9,15},{10,... | collective-permute-start | bytes 1544 | tf_op jit(solution)/shard_map/ppermute | solution.py:474
  6.5 8.0 %collective-permute-start.4 = (s32[1,128]{1,0:T(1,128)}, s32[1,128]{1,0:T(1,128)S(1)}, u32[]{:S(2)}, u32[]{:S(2)}) collective-permute-start(s32[1,128]{1,0:T(1,128)} %bitcast.23), channel_id=1, source_target_pairs={{0,5},{1,4},{2,7},{3,6},{4,1},{5,0},{6,3},{7,2},{8,13},{9,12},{10,... | collective-permute-start | bytes 1544 | tf_op jit(solution)/shard_map/ppermute | solution.py:474
  6.5 8.0 %collective-permute-start.3 = (s32[1,128]{1,0:T(1,128)}, s32[1,128]{1,0:T(1,128)S(1)}, u32[]{:S(2)}, u32[]{:S(2)}) collective-permute-start(s32[1,128]{1,0:T(1,128)} %bitcast.24), channel_id=1, source_target_pairs={{0,4},{1,5},{2,6},{3,7},{4,0},{5,1},{6,2},{7,3},{8,12},{9,13},{10,... | collective-permute-start | bytes 1544 | tf_op jit(solution)/shard_map/ppermute | solution.py:474
  8.2 6.3 %collective-permute-start.2 = (s32[1,128]{1,0:T(1,128)}, s32[1,128]{1,0:T(1,128)S(1)}, u32[]{:S(2)}, u32[]{:S(2)}) collective-permute-start(s32[1,128]{1,0:T(1,128)} %bitcast.25), channel_id=1, source_target_pairs={{0,3},{1,2},{2,1},{3,0},{4,7},{5,6},{6,5},{7,4},{8,11},{9,10},{10,... | collective-permute-start | bytes 1544 | tf_op jit(solution)/shard_map/ppermute | solution.py:474
  8.5 6.1 %collective-permute-start.1 = (s32[1,128]{1,0:T(1,128)}, s32[1,128]{1,0:T(1,128)S(1)}, u32[]{:S(2)}, u32[]{:S(2)}) collective-permute-start(s32[1,128]{1,0:T(1,128)} %bitcast.26), channel_id=1, source_target_pairs={{0,2},{1,3},{2,0},{3,1},{4,6},{5,7},{6,4},{7,5},{8,10},{9,11},{10,... | collective-permute-start | bytes 1544 | tf_op jit(solution)/shard_map/ppermute | solution.py:474
  11.5 3.0 %collective-permute-start = (s32[1,128]{1,0:T(1,128)}, s32[1,128]{1,0:T(1,128)S(1)}, u32[]{:S(2)}, u32[]{:S(2)}) collective-permute-start(s32[1,128]{1,0:T(1,128)} %bitcast.27), channel_id=1, source_target_pairs={{0,1},{1,0},{2,3},{3,2},{4,5},{5,4},{6,7},{7,6},{8,9},{9,8},{10,11... | collective-permute-start | bytes 1544 | tf_op jit(solution)/shard_map/ppermute | solution.py:474
  14.6 5.6 %collective-permute-start.7 = (bf16[136,768]{1,0:T(8,128)(2,1)}, bf16[136,768]{1,0:T(8,128)(2,1)S(1)}, u32[]{:S(2)}, u32[]{:S(2)}) collective-permute-start(bf16[136,768]{1,0:T(8,128)(2,1)} %get-tuple-element.83), channel_id=1, source_target_pairs={{0,1},{1,0},{2,3},{3,2},{4,5},{5,4},{6,7},{7,6},{8,9},{9,8},{10,11... | collective-permute-start | bytes 626696 | tf_op jit(solution)/shard_map/ppermute | solution.py:474
  15.2 6.9 %collective-permute-start.8 = (bf16[136,768]{1,0:T(8,128)(2,1)}, bf16[136,768]{1,0:T(8,128)(2,1)S(1)}, u32[]{:S(2)}, u32[]{:S(2)}) collective-permute-start(bf16[136,768]{1,0:T(8,128)(2,1)} %get-tuple-element.84), channel_id=1, source_target_pairs={{0,2},{1,3},{2,0},{3,1},{4,6},{5,7},{6,4},{7,5},{8,10},{9,11},{10,... | collective-permute-start | bytes 626696 | tf_op jit(solution)/shard_map/ppermute | solution.py:474
  15.3 35.9 %collective-permute-start.9 = (bf16[136,768]{1,0:T(8,128)(2,1)}, bf16[136,768]{1,0:T(8,128)(2,1)S(1)}, u32[]{:S(2)}, u32[]{:S(2)}) collective-permute-start(bf16[136,768]{1,0:T(8,128)(2,1)} %get-tuple-element.85), channel_id=1, source_target_pairs={{0,3},{1,2},{2,1},{3,0},{4,7},{5,6},{6,5},{7,4},{8,11},{9,10},{10,... | collective-permute-start | bytes 626696 | tf_op jit(solution)/shard_map/ppermute | solution.py:474
  16.9 34.3 %collective-permute-start.10 = (bf16[136,768]{1,0:T(8,128)(2,1)}, bf16[136,768]{1,0:T(8,128)(2,1)S(1)}, u32[]{:S(2)}, u32[]{:S(2)}) collective-permute-start(bf16[136,768]{1,0:T(8,128)(2,1)} %get-tuple-element.86), channel_id=1, source_target_pairs={{0,4},{1,5},{2,6},{3,7},{4,0},{5,1},{6,2},{7,3},{8,12},{9,13},{10,... | collective-permute-start | bytes 626696 | tf_op jit(solution)/shard_map/ppermute | solution.py:474
  18.0 33.2 %collective-permute-start.11 = (bf16[136,768]{1,0:T(8,128)(2,1)}, bf16[136,768]{1,0:T(8,128)(2,1)S(1)}, u32[]{:S(2)}, u32[]{:S(2)}) collective-permute-start(bf16[136,768]{1,0:T(8,128)(2,1)} %get-tuple-element.87), channel_id=1, source_target_pairs={{0,5},{1,4},{2,7},{3,6},{4,1},{5,0},{6,3},{7,2},{8,13},{9,12},{10,... | collective-permute-start | bytes 626696 | tf_op jit(solution)/shard_map/ppermute | solution.py:474
  20.2 31.0 %collective-permute-start.12 = (bf16[136,768]{1,0:T(8,128)(2,1)}, bf16[136,768]{1,0:T(8,128)(2,1)S(1)}, u32[]{:S(2)}, u32[]{:S(2)}) collective-permute-start(bf16[136,768]{1,0:T(8,128)(2,1)} %get-tuple-element.88), channel_id=1, source_target_pairs={{0,6},{1,7},{2,4},{3,5},{4,2},{5,3},{6,0},{7,1},{8,14},{9,15},{10,... | collective-permute-start | bytes 626696 | tf_op jit(solution)/shard_map/ppermute | solution.py:474
  22.1 29.1 %collective-permute-start.13 = (bf16[136,768]{1,0:T(8,128)(2,1)}, bf16[136,768]{1,0:T(8,128)(2,1)S(1)}, u32[]{:S(2)}, u32[]{:S(2)}) collective-permute-start(bf16[136,768]{1,0:T(8,128)(2,1)} %get-tuple-element.89), channel_id=1, source_target_pairs={{0,7},{1,6},{2,5},{3,4},{4,3},{5,2},{6,1},{7,0},{8,15},{9,14},{10,... | collective-permute-start | bytes 626696 | tf_op jit(solution)/shard_map/ppermute | solution.py:474
  24.4 0.7 copy-start
  25.0 0.7 copy-start.2
  36.3 14.8 %all-to-all-start.2 = ((s32[8,4,128]{2,1,0:T(4,128)}), s32[8,4,128]{2,1,0:T(4,128)S(1)}, u32[]{:S(2)}, u32[]{:S(2)}) async-start(s32[8,4,128]{2,1,0:T(4,128)} %copy.13), calls=%async_computation.2 | async-start | bytes 32768 | tf_op jit(solution)/shard_map/all_to_all | solution.py:466
  56.6 65.9 %copy-start.1 = (s32[1024]{0:T(1024)S(1)}, s32[1024]{0:T(1024)}, u32[]{:S(2)}) copy-start(s32[1024]{0:T(1024)} %segment_ref.1) | copy-start | bytes 12292

commit v3 on v2

--- a/solution.py
+++ b/solution.py
@@ -17,6 +17,8 @@
 WIDTH = 6 * HEAD_DIM
 LANES = 128
 BLOCK = 256
+GATHER = 512
+SEND = 16
 CAPACITY = 56
 EXTRA = 16
 
@@ -39,9 +41,10 @@
     return jnp.dot(left, right, preferred_element_type=jnp.float32)
 
 
-def pack_kernel(me_ref, query_hbm, key_hbm, value_hbm, out_hbm, grad_hbm, *refs):
-    packed_refs = refs[:N_SEQ]
-    query_ref, key_ref, value_ref, out_ref, grad_ref, delta_ref, sems = refs[N_SEQ:]
+def pack_kernel(
+    query_hbm, key_hbm, value_hbm, out_hbm, grad_hbm, packed_ref,
+    query_ref, key_ref, value_ref, out_ref, grad_ref, sems,
+):
     pairs = (
         (grad_hbm, grad_ref),
         (out_hbm, out_ref),
@@ -57,33 +60,32 @@
         copy.start()
     copies[0].wait()
     copies[1].wait()
+    columns = []
+    for head in range(2 * N_SEQ):
+        cols = slice(head * HEAD_DIM, (head + 1) * HEAD_DIM)
+        product = grad_ref[:, cols].astype(jnp.float32) * out_ref[:, cols].astype(jnp.float32)
+        columns.append(jnp.sum(product, axis=1, keepdims=True))
     lane = iota((ROWS, LANES), 1)
     table = jnp.zeros((ROWS, LANES), jnp.float32)
     for head in range(2 * N_SEQ):
-        cols = slice(head * HEAD_DIM, (head + 1) * HEAD_DIM)
-        product = grad_ref[:, cols].astype(jnp.float32) * out_ref[:, cols].astype(jnp.float32)
-        table = jnp.where(lane == head, jnp.sum(product, axis=1, keepdims=True), table)
+        table = jnp.where(lane == head, columns[head], table)
     delta = table.T
     high = delta.astype(jnp.bfloat16).astype(jnp.float32)
     low = delta - high
-    for group in range(N_SEQ):
-        pair = slice(2 * group, 2 * group + 2)
-        delta_ref[group] = jnp.concatenate(
-            [high[pair], low[pair], jnp.zeros((4, LANES), jnp.float32)], axis=0
-        )
+    pad_rows = jnp.zeros((4, LANES), jnp.float32)
     pad_cols = jnp.zeros((8, WIDTH - LANES), jnp.float32)
     for copy in copies[2:]:
         copy.wait()
-    me = me_ref[0]
-    for m in range(N_SEQ):
-        group = jnp.bitwise_xor(me, m)
-        two = pl.ds(pl.multiple_of(group * 256, 256), 256)
-        one = pl.ds(pl.multiple_of(group * 128, 128), 128)
+    for group in range(N_SEQ):
+        two = slice(2 * group * HEAD_DIM, 2 * (group + 1) * HEAD_DIM)
+        one = slice(group * HEAD_DIM, (group + 1) * HEAD_DIM)
+        pair = slice(2 * group, 2 * group + 2)
         rows = jnp.concatenate(
             [query_ref[:, two], key_ref[:, one], value_ref[:, one], grad_ref[:, two]], axis=1
         )
-        extra = jnp.concatenate([delta_ref[group], pad_cols], axis=1)
-        packed_refs[m][...] = jnp.concatenate([rows.astype(jnp.float32), extra], axis=0).astype(
+        extra = jnp.concatenate([high[pair], low[pair], pad_rows], axis=0)
+        extra = jnp.concatenate([extra, pad_cols], axis=1)
+        packed_ref[group] = jnp.concatenate([rows.astype(jnp.float32), extra], axis=0).astype(
             jnp.bfloat16
         )
 
@@ -92,10 +94,11 @@
     return jnp.concatenate([rows[s : s + 1] for s in range(N_SEQ)], axis=1)
 
 
-def index_kernel(me_ref, segment_ref, *refs):
-    lists, (rows_ref, cols_ref, request_ref, most_ref, list_ref) = refs[:N_SEQ], refs[N_SEQ:]
+def index_kernel(ids_ref, segment_ref, *refs):
+    lists, (rows_ref, cols_ref), refs = refs[:N_SEQ], refs[N_SEQ : N_SEQ + 2], refs[N_SEQ + 2 :]
+    tables, (most_ref, list_ref, table_ref) = refs[:N_X], refs[N_X:]
     for m in range(N_SEQ):
-        list_ref[pl.ds(jnp.bitwise_xor(me_ref[0], m), 1), :] = lists[m][...]
+        list_ref[pl.ds(jnp.bitwise_xor(ids_ref[0], m), 1), :] = lists[m][...]
     listed = list_ref[...]
     source = (listed // GROUP).astype(jnp.float32)
     local_row = (listed % ROWS).astype(jnp.float32)
@@ -125,66 +128,78 @@
     rows_ref[8:16, :] = slot
     rows_ref[16:24, :] = segment
     pick = jnp.concatenate(picks, axis=0).astype(jnp.bfloat16)
-    from_source = iota((N_DP, GROUP), 0).astype(jnp.float32) == wide(source)
+    place = iota((N_DP, GROUP), 0)
+    place = (place % N_Z) * N_X + place // N_Z
+    from_source = place.astype(jnp.float32) == wide(source)
     column = (iota((1, GROUP), 1) // ROWS).astype(jnp.float32)
     low = jnp.where(from_source, wide(local_row) + 1.0, 0.0).astype(jnp.bfloat16)
     high = jnp.where(from_source, column, 0.0).astype(jnp.bfloat16)
     table = nn_dot(low, pick) + float(ROWS) * nn_dot(high, pick)
-    request_ref[...] = table.astype(jnp.int32)
+    for x in range(N_X):
+        table_ref[x] = table[x * N_Z : (x + 1) * N_Z].astype(jnp.int32)
+    for m in range(N_X):
+        tables[m][...] = table_ref[jnp.bitwise_xor(ids_ref[1], m)]
     most_ref[0, 0] = (jnp.max(slot) + 1.0).astype(jnp.int32)
 
 
-def turned_requests(request_ref):
+def turn_kernel(ids_ref, *refs):
+    tables, turned = refs[:N_X], refs[N_X:]
+    for m in range(N_X):
+        x = jnp.bitwise_xor(ids_ref[1], m)
+        for n in range(N_Z):
+            z = jnp.bitwise_xor(ids_ref[2], n)
+            turned[n][pl.ds(x, 1), :] = tables[m][pl.ds(z, 1), :]
+
+
+def turned_requests(ids_ref, tables, request_ref):
+    for n in range(N_Z):
+        request_ref[jnp.bitwise_xor(ids_ref[2], n)] = tables[n][...].astype(jnp.float32)
     blank = jnp.zeros((LANES - N_DP, LANES), jnp.float32)
-    return jnp.concatenate([request_ref[...].astype(jnp.float32), blank], axis=0).T - 1.0
+    return jnp.concatenate([request_ref[z] for z in range(N_Z)] + [blank], axis=0).T - 1.0
 
 
 def group_picks(turned, group, first, capacity):
-    column = jnp.concatenate(
-        [turned[first : first + capacity, d : d + 1] for d in range(8 * group, 8 * group + 8)], axis=0
-    )
-    row_id = iota((8 * capacity, GROUP), 1).astype(jnp.float32)
+    owners = range(SEND * group, SEND * (group + 1))
+    column = jnp.concatenate([turned[first : first + capacity, d : d + 1] for d in owners], axis=0)
+    row_id = iota((SEND * capacity, GROUP), 1).astype(jnp.float32)
     return (column == row_id).astype(jnp.float32).astype(jnp.bfloat16)
 
 
-def join_columns(me_ref, parts, ext_ref, delta_ref):
-    for m in range(N_SEQ):
-        column = jnp.bitwise_xor(me_ref[0], m)
-        whole = parts[m][...]
-        ext_ref[pl.ds(pl.multiple_of(column * ROWS, ROWS), ROWS), :] = whole[:ROWS]
-        if delta_ref is not None:
-            delta_ref[column] = whole[ROWS:, :LANES].astype(jnp.float32)
-
-
-def send_extra_kernel(me_ref, request_ref, *refs):
-    parts, (sent_ref, ext_ref) = refs[:N_SEQ], refs[N_SEQ:]
-    group_rows = 8 * EXTRA
-    turned = turned_requests(request_ref)
-    join_columns(me_ref, parts, ext_ref, None)
-    for group in range(N_DP // 8):
+def send_extra_kernel(ids_ref, *refs):
+    tables, (rows_ref, sent_ref, ext_ref, request_ref) = refs[:N_Z], refs[N_Z:]
+    group_rows = SEND * EXTRA
+    turned = turned_requests(ids_ref, tables, request_ref)
+    for s in range(N_SEQ):
+        whole = rows_ref[s]
+        ext_ref[s * ROWS : (s + 1) * ROWS, :] = whole[:ROWS]
+    for group in range(N_DP // SEND):
         pick = group_picks(turned, group, CAPACITY, EXTRA)
         rows = slice(group * group_rows, (group + 1) * group_rows)
         sent_ref[rows, :] = nn_dot(pick, ext_ref[...]).astype(jnp.bfloat16)
 
 
-def send_kernel(me_ref, most_ref, request_ref, *refs):
-    parts, (sent_ref, ext_ref, place_ref, delta_ref) = refs[:N_SEQ], refs[N_SEQ:]
+def send_kernel(ids_ref, most_ref, *refs):
+    tables, (rows_ref, sent_ref, ext_ref, place_ref, request_ref) = refs[:N_Z], refs[N_Z:]
     capacity = CAPACITY
-    group_rows = 8 * capacity
-    turned = turned_requests(request_ref)
-    join_columns(me_ref, parts, ext_ref, delta_ref)
-    delta = jnp.concatenate([delta_ref[s] for s in range(N_SEQ)], axis=1)
+    group_rows = SEND * capacity
+    turned = turned_requests(ids_ref, tables, request_ref)
+    deltas = []
+    for s in range(N_SEQ):
+        whole = rows_ref[s]
+        ext_ref[s * ROWS : (s + 1) * ROWS, :] = whole[:ROWS]
+        deltas.append(whole[ROWS:, :LANES].astype(jnp.float32))
+    delta = jnp.concatenate(deltas, axis=1)
 
     def places(pick, group, first, count):
-        index = iota((8, 8 * count), 1)
+        index = iota((8, SEND * count), 1)
         owner = index // count
         value = jnp.where(
-            iota((8, 8 * count), 0) == 0, owner + 8 * group, index - owner * count + first
+            iota((8, SEND * count), 0) == 0, owner + SEND * group, index - owner * count + first
         )
         return nn_dot(value.astype(jnp.float32).astype(jnp.bfloat16), pick)
 
     place = jnp.zeros((8, GROUP), jnp.float32)
-    for group in range(N_DP // 8):
+    for group in range(N_DP // SEND):
         pick = group_picks(turned, group, 0, capacity)
         place = place + places(pick, group, 0, capacity)
         rows = slice(group * group_rows, (group + 1) * group_rows)
@@ -194,7 +209,7 @@
     @pl.when(most_ref[0, 0] >= CAPACITY)
     def _():
         more = jnp.zeros((8, GROUP), jnp.float32)
-        for group in range(N_DP // 8):
+        for group in range(N_DP // SEND):
             more = more + places(group_picks(turned, group, CAPACITY, EXTRA), group, CAPACITY, EXTRA)
         place_ref[...] += more
 
@@ -231,9 +246,9 @@
 ):
     slots = N_DP * CAPACITY
     blocks = GROUP // BLOCK
-    slot_id = iota((BLOCK, slots), 1).astype(jnp.float32)
-    for block in range(blocks):
-        rows = slice(block * BLOCK, (block + 1) * BLOCK)
+    slot_id = iota((GATHER, slots), 1).astype(jnp.float32)
+    for block in range(GROUP // GATHER):
+        rows = slice(block * GATHER, (block + 1) * GATHER)
         slot = cols_ref[rows, 1:2] + 1.0
         place = jnp.where(slot < CAPACITY, cols_ref[rows, 0:1] * float(CAPACITY) + slot, -1.0)
         pick = (place == slot_id).astype(jnp.float32).astype(jnp.bfloat16)
@@ -359,44 +374,54 @@
     return pl.CostEstimate(flops=flops, bytes_accessed=moved, transcendentals=transcendentals)
 
 
-def pack(me, query, key_rows, value_rows, attn_out, out_grad):
+def pack(query, key_rows, value_rows, attn_out, out_grad):
     return pl.pallas_call(
         pack_kernel,
-        out_shape=[shape((ROWS + 8, WIDTH))] * N_SEQ,
-        in_specs=[SMEM] + [pl.BlockSpec(memory_space=pltpu.HBM)] * 5,
-        out_specs=[VMEM] * N_SEQ,
+        out_shape=shape((N_SEQ, ROWS + 8, WIDTH)),
+        in_specs=[pl.BlockSpec(memory_space=pltpu.HBM)] * 5,
+        out_specs=VMEM,
         scratch_shapes=[
             pltpu.VMEM((ROWS, 2048), jnp.bfloat16),
             pltpu.VMEM((ROWS, 1024), jnp.bfloat16),
             pltpu.VMEM((ROWS, 1024), jnp.bfloat16),
             pltpu.VMEM((ROWS, 2048), jnp.bfloat16),
             pltpu.VMEM((ROWS, 2048), jnp.bfloat16),
-            pltpu.VMEM((N_SEQ, 8, LANES), jnp.float32),
             pltpu.SemaphoreType.DMA((5,)),
         ],
         compiler_params=FULL,
         name="pack",
-    )(me, query, key_rows, value_rows, attn_out, out_grad)
-
-
-def index(me, segments, lists):
+    )(query, key_rows, value_rows, attn_out, out_grad)
+
+
+def index(ids, segments, lists):
     return pl.pallas_call(
         index_kernel,
-        out_shape=(
-            shape((24, LANES), jnp.float32),
-            shape((GROUP, LANES), jnp.float32),
-            shape((N_DP, LANES), jnp.int32),
-            shape((1, 1), jnp.int32),
-        ),
+        out_shape=[shape((24, LANES), jnp.float32), shape((GROUP, LANES), jnp.float32)]
+        + [shape((N_Z, LANES), jnp.int32)] * N_X
+        + [shape((1, 1), jnp.int32)],
         in_specs=[SMEM] + [VMEM] * 9,
-        out_specs=(VMEM, VMEM, VMEM, SMEM),
-        scratch_shapes=[pltpu.VMEM((N_SEQ, LANES), jnp.int32)],
+        out_specs=[VMEM] * (2 + N_X) + [SMEM],
+        scratch_shapes=[
+            pltpu.VMEM((N_SEQ, LANES), jnp.int32),
+            pltpu.VMEM((N_X, N_Z, LANES), jnp.int32),
+        ],
         compiler_params=PARAMS,
         name="index",
-    )(me, segments.reshape(N_SEQ, ROWS), *lists)
-
-
-def send(me, most, request, parts):
+    )(ids, segments.reshape(N_SEQ, ROWS), *lists)
+
+
+def turn(ids, tables):
+    return pl.pallas_call(
+        turn_kernel,
+        out_shape=[shape((N_X, LANES), jnp.int32)] * N_Z,
+        in_specs=[SMEM] + [VMEM] * N_X,
+        out_specs=[VMEM] * N_Z,
+        compiler_params=PARAMS,
+        name="turn",
+    )(ids, *tables)
+
+
+def send(ids, most, tables, head_rows):
     return pl.pallas_call(
         send_kernel,
         out_shape=shape((N_DP * CAPACITY, WIDTH)),
@@ -404,23 +429,25 @@
         scratch_shapes=[
             pltpu.VMEM((GROUP, WIDTH), jnp.bfloat16),
             pltpu.VMEM((8, GROUP), jnp.float32),
-            pltpu.VMEM((N_SEQ, 8, LANES), jnp.float32),
+            pltpu.VMEM((N_Z, N_X, LANES), jnp.float32),
         ],
         compiler_params=PARAMS,
-        cost_estimate=cost(2 * N_DP * CAPACITY * GROUP * WIDTH, 4_000_000),
         name="send",
-    )(me, most, request, *parts)
-
-
-def send_extra(me, request, parts):
+    )(ids, most, *tables, head_rows)
+
+
+def send_extra(ids, tables, head_rows):
     return pl.pallas_call(
         send_extra_kernel,
         out_shape=shape((N_DP * EXTRA, WIDTH)),
         in_specs=[SMEM] + [VMEM] * 9,
-        scratch_shapes=[pltpu.VMEM((GROUP, WIDTH), jnp.bfloat16)],
+        scratch_shapes=[
+            pltpu.VMEM((GROUP, WIDTH), jnp.bfloat16),
+            pltpu.VMEM((N_Z, N_X, LANES), jnp.float32),
+        ],
         compiler_params=PARAMS,
         name="send_extra",
-    )(me, request, *parts)
+    )(ids, *tables, head_rows)
 
 
 def attend(segments, most, arrived, extra, rows, cols):
@@ -457,35 +484,31 @@
     return lax.all_to_all(array, "dp", split_axis=0, concat_axis=0, tiled=True)
 
 
-def relay_requests(request):
-    along_x = [[z * N_X + x for x in range(N_X)] for z in range(N_Z)]
-    along_z = [[z * N_X + x for z in range(N_Z)] for x in range(N_X)]
-    request = request.reshape(N_Z, N_X, LANES).transpose(1, 0, 2)
-    request = lax.all_to_all(request, "dp", 0, 0, axis_index_groups=along_x, tiled=True)
-    request = request.transpose(1, 0, 2)
-    request = lax.all_to_all(request, "dp", 0, 0, axis_index_groups=along_z, tiled=True)
-    return request.reshape(N_DP, LANES)
+def swap_seq(array, m):
+    return lax.ppermute(array, "seq", [(s, s ^ m) for s in range(N_SEQ)]) if m else array
+
+
+def swap_dp(array, m):
+    return lax.ppermute(array, "dp", [(d, d ^ m) for d in range(N_DP)]) if m else array
 
 
 def local(query, key_rows, value_rows, attn_out, out_grad, source_row, segment_ids):
-    me = lax.axis_index("seq").reshape(1)
-
-    def swap(array, m):
-        return lax.ppermute(array, "seq", [(s, s ^ m) for s in range(N_SEQ)]) if m else array
-
-    lists = [swap(source_row.reshape(1, ROWS), m) for m in range(N_SEQ)]
-    packed = pack(me, query, key_rows, value_rows, attn_out, out_grad)
+    my_dp = lax.axis_index("dp")
+    ids = jnp.stack([lax.axis_index("seq"), my_dp % N_X, my_dp // N_X])
+    lists = [swap_seq(source_row.reshape(1, ROWS), m) for m in range(N_SEQ)]
+    packed = pack(query, key_rows, value_rows, attn_out, out_grad)
     packed, lists = lax.optimization_barrier((packed, lists))
-    parts = [swap(packed[m], m) for m in range(N_SEQ)]
-    rows, cols, request, most = index(me, segment_ids, lists)
-    request = relay_requests(request)
-    arrived = relay(send(me, most, request, parts))
+    head_rows = lax.all_to_all(packed, "seq", split_axis=0, concat_axis=0, tiled=True)
+    rows, cols, *tables, most = index(ids, segment_ids, lists)
+    tables = turn(ids, [swap_dp(tables[m], m) for m in range(N_X)])
+    tables = [swap_dp(tables[n], n * N_X) for n in range(N_Z)]
+    arrived = relay(send(ids, most, tables, head_rows))
     extra = lax.cond(
         most[0, 0] >= CAPACITY,
-        lambda request, *parts: relay(send_extra(me, request, parts)),
-        lambda request, *parts: jnp.zeros((N_DP * EXTRA, WIDTH), jnp.bfloat16),
-        request,
-        *parts,
+        lambda tables, head_rows: relay(send_extra(ids, tables, head_rows)),
+        lambda tables, head_rows: jnp.zeros((N_DP * EXTRA, WIDTH), jnp.bfloat16),
+        tables,
+        head_rows,
     )
     grads = attend(segment_ids, most, arrived, extra, rows, cols)
     returned = lax.all_to_all(

time: 155 us -> 153 us (0.987)
  starting transfers between devices: 28 us -> 33.4 us
  blocking collectives: 94.8 us -> 89.5 us
  local copies, waits for them, and re-layouts: 2.02 us -> 0.06 us
    ppermute x14 -> x17, starting transfers between devices: 19.8 us -> 29.4 us  [the longest x10 18.5 us: swap_dp(): lax.ppermute(array, 'dp', [(d, d ^ m) for d in range(N_DP)])]
    all_to_all x1 -> x0, blocking collectives: 8.32 us -> none  [relay_requests(): lax.all_to_all(request, 'dp', 0, 0, axis_index_groups=along_x, tiled=True)]
    all_to_all x1, waiting for transfers between devices: 5.97 us -> 0.01 us  [local(): lax.all_to_all(packed, 'seq', split_axis=0, concat_axis=0, tiled=True)]
    ppermute x14 -> x17, waiting for transfers between devices: 0.9 us -> 5.56 us  [the longest x10 5.54 us: swap_dp(): lax.ppermute(array, 'dp', [(d, d ^ m) for d in range(N_DP)])]
    all_to_all x1, blocking collectives: 20.6 us -> 25 us  [local(): lax.all_to_all(grads.reshape(N_SEQ, ROWS, 4 * HEAD_DIM), 'seq', split_axi...]
    all_to_all x1, starting transfers between devices: 8.19 us -> 4 us  [local(): lax.all_to_all(packed, 'seq', split_axis=0, concat_axis=0, tiled=True)]
    pallas_call x2 -> x3, Pallas kernels: 4.66 us -> 5.76 us  [the longest x1 3.01 us: pack(): pl.pallas_call(pack_kernel, out_shape=shape((N_SEQ, ROWS + 8, WIDTH)), in...]
  transfers between devices with their start and end apart: 15 -> 18, of which waited for: 2 -> 4; matrix products, arithmetic and copies ran while one was open for 0% -> 0% of each run, Pallas kernels for 3% -> 4%
where the time goes in v3:
time: 153 us
  blocking collectives  89.5 us (58%)
  starting transfers between devices  33.4 us (22%)
  Pallas kernels  23 us (15%)
  waiting for transfers between devices  5.56 us (4%)
    all_to_all x1, blocking collectives, relay(): return lax.all_to_all(array, 'dp', split_axis=0, concat_axis=0, tiled=True)  64.6 us
    all_to_all x1, blocking collectives, local(): lax.all_to_all(grads.reshape(N_SEQ, ROWS, 4 * HEAD_DIM), 'seq', split_axi...  25 us
    ppermute x10, starting transfers between devices, swap_dp(): lax.ppermute(array, 'dp', [(d, d ^ m) for d in range(N_DP)])  18.5 us
    ppermute x7, starting transfers between devices, swap_seq(): lax.ppermute(array, 'seq', [(s, s ^ m) for s in range(N_SEQ)])  10.9 us
    pallas_call x1, Pallas kernels, attend(): pl.pallas_call(attend_kernel, out_shape=shape((GROUP, 4 * HEAD_DIM)), in_...  10.3 us
    pallas_call x1, Pallas kernels, send(): pl.pallas_call(send_kernel, out_shape=shape((N_DP * CAPACITY, WIDTH)), in...  5.8 us
    ppermute x10, waiting for transfers between devices, swap_dp(): lax.ppermute(array, 'dp', [(d, d ^ m) for d in range(N_DP)])  5.54 us
    all_to_all x1, starting transfers between devices, local(): lax.all_to_all(packed, 'seq', split_axis=0, concat_axis=0, tiled=True)  4 us
  transfers between devices with their start and end apart: 18, of which 4 were waited for; matrix products, arithmetic and copies ran while one was open for 0% of the time, Pallas kernels for 4%

profile of v3, /device:TPU:1, one launch (start us, length us, event | category | flops | bytes accessed | tf_op | source)
XLA Modules:
  0.0 153.3 jit_solution(14652740342193718060)
XLA Ops:
  0.6 0.0 copy-start
  0.6 0.0 copy-start.1
  0.7 4.2 %collective-permute-start.6 = (s32[1,128]{1,0:T(1,128)}, s32[1,128]{1,0:T(1,128)S(1)}, u32[]{:S(2)}, u32[]{:S(2)}) collective-permute-start(s32[1,128]{1,0:T(1,128)} %bitcast.16), channel_id=1, source_target_pairs={{0,7},{1,6},{2,5},{3,4},{4,3},{5,2},{6,1},{7,0},{8,15},{9,14},{10,... | collective-permute-start | bytes 1544 | tf_op jit(solution)/shard_map/ppermute | solution.py:488
  4.9 1.7 %collective-permute-start.5 = (s32[1,128]{1,0:T(1,128)}, s32[1,128]{1,0:T(1,128)S(1)}, u32[]{:S(2)}, u32[]{:S(2)}) collective-permute-start(s32[1,128]{1,0:T(1,128)} %bitcast.17), channel_id=1, source_target_pairs={{0,6},{1,7},{2,4},{3,5},{4,2},{5,3},{6,0},{7,1},{8,14},{9,15},{10,... | collective-permute-start | bytes 1544 | tf_op jit(solution)/shard_map/ppermute | solution.py:488
  6.5 0.0 collective-permute-start.4
  6.5 1.7 %collective-permute-start.3 = (s32[1,128]{1,0:T(1,128)}, s32[1,128]{1,0:T(1,128)S(1)}, u32[]{:S(2)}, u32[]{:S(2)}) collective-permute-start(s32[1,128]{1,0:T(1,128)} %bitcast.19), channel_id=1, source_target_pairs={{0,4},{1,5},{2,6},{3,7},{4,0},{5,1},{6,2},{7,3},{8,12},{9,13},{10,... | collective-permute-start | bytes 1544 | tf_op jit(solution)/shard_map/ppermute | solution.py:488
  8.2 0.3 collective-permute-start.2
  8.5 0.0 collective-permute-done.6.refs_7_
  8.5 3.1 %collective-permute-start.1 = (s32[1,128]{1,0:T(1,128)}, s32[1,128]{1,0:T(1,128)S(1)}, u32[]{:S(2)}, u32[]{:S(2)}) collective-permute-start(s32[1,128]{1,0:T(1,128)} %bitcast.21), channel_id=1, source_target_pairs={{0,2},{1,3},{2,0},{3,1},{4,6},{5,7},{6,4},{7,5},{8,10},{9,11},{10,... | collective-permute-start | bytes 1544 | tf_op jit(solution)/shard_map/ppermute | solution.py:488
  11.5 0.0 collective-permute-done.5.refs_6_
  11.5 0.0 collective-permute-start
  11.6 3.0 %pack.1 = bf16[8,136,768]{2,1,0:T(8,128)(2,1)} custom-call(bf16[128,2048]{1,0:T(8,128)(2,1)} %query_hbm.1, bf16[128,1024]{1,0:T(8,128)(2,1)} %key_hbm.1, bf16[128,1024]{1,0:T(8,128)(2,1)} %value_hbm.1, bf16[128,2048]{1,0:T(8,128)(2,1)} %out_hbm.1, bf16[128,2048]{1,0:T(8,128)(2,1)} %grad_hbm.1), custom_call_target="tpu_custom_call" | custom-call | tf_op jit(solution)/shard_map/pack/pallas_call | solution.py:378
  14.6 0.0 collective-permute-done.4.refs_5_
  14.6 0.0 collective-permute-done.3.refs_4_
  14.6 0.0 collective-permute-done.2.refs_3_
  14.6 0.0 collective-permute-done.1.refs_2_
  14.6 0.0 collective-permute-done.refs_1_
  14.6 4.0 %all-to-all-start.1 = ((bf16[8,136,768]{2,1,0:T(8,128)(2,1)}), bf16[8,136,768]{2,1,0:T(8,128)(2,1)S(1)}, u32[]{:S(2)}, u32[]{:S(2)}) async-start(bf16[8,136,768]{2,1,0:T(8,128)(2,1)} %pack.1), calls=%async_computation.1 | async-start | bytes 3342336 | tf_op jit(solution)/shard_map/all_to_all | solution.py:501
  18.6 0.1 pad_add_fusion.ids_ref
  18.7 0.0 copy-done
  18.7 0.0 copy-done.1
  18.7 2.2 %index.1 = (f32[24,128]{1,0:T(8,128)S(1)}, f32[1024,128]{1,0:T(8,128)S(1)}, s32[8,128]{1,0:T(8,128)S(1)}, s32[8,128]{1,0:T(8,128)S(1)}, s32[8,128]{1,0:T(8,128)S...) custom-call(s32[3]{0:T(128)S(1)} %pad_add_fusion.ids_ref, s32[8,128]{1,0:T(8,128)S(1)} %bitcast.15, s32[1,128]{1,0:T(1,128)S(1)} %bitcast.23, ...), custom_call_target="tpu_custom_call" | custom-call | tf_op jit(solution)/shard_map/index/pallas_call | solution.py:397
  20.9 0.4 collective-permute-start.7
  21.3 2.5 %collective-permute-start.8 = (s32[8,128]{1,0:T(8,128)S(1)}, s32[8,128]{1,0:T(8,128)S(1)}, u32[]{:S(2)}, u32[]{:S(2)}) collective-permute-start(s32[8,128]{1,0:T(8,128)S(1)} %get-tuple-element.71), channel_id=1, source_target_pairs={{0,16},{8,24},{16,0},{24,8},{32,48},{40,56},{48,32},{56,40},{64,80... | collective-permute-start | bytes 12296 | tf_op jit(solution)/shard_map/ppermute | solution.py:492
  23.7 1.1 collective-permute-start.9
  24.8 0.0 collective-permute-done.7.refs_1_
  24.8 0.7 collective-permute-done.8.refs_2_
  25.5 1.9 %collective-permute-done.9.refs_3_ = s32[8,128]{1,0:T(8,128)S(1)} collective-permute-done((s32[8,128]{1,0:T(8,128)S(1)}, s32[8,128]{1,0:T(8,128)S(1)}, u32[]{:S(2)}, u32[]{:S(2)}) %collective-permute-start.9) | collective-permute-done | bytes 4128 | tf_op jit(solution)/shard_map/ppermute | solution.py:492
  27.4 0.6 turn.1
  28.0 1.7 %collective-permute-start.10 = (s32[4,128]{1,0:T(4,128)S(1)}, s32[4,128]{1,0:T(4,128)S(1)}, u32[]{:S(2)}, u32[]{:S(2)}) collective-permute-start(s32[4,128]{1,0:T(4,128)S(1)} %get-tuple-element.74), channel_id=1, source_target_pairs={{0,32},{8,40},{16,48},{24,56},{32,0},{40,8},{48,16},{56,24},{64,96... | collective-permute-start | bytes 6152 | tf_op jit(solution)/shard_map/ppermute | solution.py:492
  29.7 3.0 %collective-permute-start.11 = (s32[4,128]{1,0:T(4,128)S(1)}, s32[4,128]{1,0:T(4,128)S(1)}, u32[]{:S(2)}, u32[]{:S(2)}) collective-permute-start(s32[4,128]{1,0:T(4,128)S(1)} %get-tuple-element.75), channel_id=1, source_target_pairs={{0,64},{8,72},{16,80},{24,88},{32,96},{40,104},{48,112},{56,120},{... | collective-permute-start | bytes 6152 | tf_op jit(solution)/shard_map/ppermute | solution.py:492
  32.7 0.0 collective-permute-start.12
  32.7 5.8 %collective-permute-start.13 = (s32[4,128]{1,0:T(4,128)S(1)}, s32[4,128]{1,0:T(4,128)S(1)}, u32[]{:S(2)}, u32[]{:S(2)}) collective-permute-start(s32[4,128]{1,0:T(4,128)S(1)} %get-tuple-element.77), channel_id=1, source_target_pairs={{0,128},{8,136},{16,144},{24,152},{32,160},{40,168},{48,176},{56,1... | collective-permute-start | bytes 6152 | tf_op jit(solution)/shard_map/ppermute | solution.py:492
  38.5 0.0 collective-permute-start.14
  38.5 0.0 collective-permute-done.10.refs_1_
  38.5 4.0 %collective-permute-start.15 = (s32[4,128]{1,0:T(4,128)S(1)}, s32[4,128]{1,0:T(4,128)S(1)}, u32[]{:S(2)}, u32[]{:S(2)}) collective-permute-start(s32[4,128]{1,0:T(4,128)S(1)} %get-tuple-element.79), channel_id=1, source_target_pairs={{0,192},{8,200},{16,208},{24,216},{32,224},{40,232},{48,240},{56,2... | collective-permute-start | bytes 6152 | tf_op jit(solution)/shard_map/ppermute | solution.py:492
  42.6 0.0 collective-permute-done.11.refs_2_
  42.6 0.0 collective-permute-start.16
  43.2 0.0 collective-permute-done.12.refs_3_
  43.2 0.0 collective-permute-done.13.refs_4_
  43.3 0.7 collective-permute-done.14.refs_5_
  44.0 0.0 collective-permute-done.15.refs_6_
  44.0 2.2 %collective-permute-done.16.refs_7_ = s32[4,128]{1,0:T(4,128)S(1)} collective-permute-done((s32[4,128]{1,0:T(4,128)S(1)}, s32[4,128]{1,0:T(4,128)S(1)}, u32[]{:S(2)}, u32[]{:S(2)}) %collective-permute-start.16) | collective-permute-done | bytes 2080 | tf_op jit(solution)/shard_map/ppermute | solution.py:492
  46.2 0.0 all-to-all-done.1.refs_8_
  46.2 0.2 conditional.1
  46.2 0.1 broadcast.4
  46.5 5.8 %send.1 = bf16[1792,768]{1,0:T(8,128)(2,1)S(1)} custom-call(s32[3]{0:T(128)S(1)} %pad_add_fusion.ids_ref, s32[1,1]{1,0:T(1,128)} %get-tuple-element.68.most_ref, s32[4,128]{1,0:T(4,128)S(1)} %get-tuple-element.73.refs_0_, s32[4,128]{1,0:T(4,128)S(1)} %collective-permute-done.10.refs_1_, s32[4,128]{1,0:T(4,128)S(1)} %collective-permute-done.11.refs_2_, ...), custom_call_target="tpu_custom_call" | custom-call | tf_op jit(solution)/shard_map/send/pallas_call | solution.py:425
  52.3 64.6 %all_to_all.31 = bf16[32,56,768]{2,1,0:T(8,128)(2,1)S(1)} all-to-all(bf16[32,56,768]{2,1,0:T(8,128)(2,1)S(1)} %bitcast.11), channel_id=1, replica_groups=mesh['dp'=32,'seq'=8] {'dp'}, dimensions={0} | all-to-all | bytes 5505024 | tf_op jit(solution)/shard_map/all_to_all | solution.py:484
  116.8 10.3 %attend.1 = bf16[1024,512]{1,0:T(8,128)(2,1)S(1)} custom-call(s32[1024]{0:T(1024)S(1)} %copy-done, s32[1,1]{1,0:T(1,128)} %get-tuple-element.68.most_ref, bf16[1792,768]{1,0:T(8,128)(2,1)S(1)} %bitcast.12, bf16[512,768]{1,0:T(8,128)(2,1)S(1)} %get-tuple-element.84.extra_ref, f32[24,128]{1,0:T(8,128)S(1)} %get-tuple-element.82.rows_ref, ...), custom_call_target="tpu_custom_call" | custom-call | tf_op jit(solution)/shard_map/attend/pallas_call | solution.py:454
  127.2 25.0 %all_to_all.32.returned_ref = bf16[8,128,512]{2,1,0:T(8,128)(2,1)S(1)} all-to-all(bf16[8,128,512]{2,1,0:T(8,128)(2,1)S(1)} %bitcast.13), channel_id=1, replica_groups=mesh['dp'=32,'seq'=8] {'seq'}, dimensions={0} | all-to-all | bytes 2097152 | tf_op jit(solution)/shard_map/all_to_all | solution.py:514
  152.1 1.2 unpack.1
Async XLA Ops:
  0.6 18.1 %copy-start = (s32[1024]{0:T(1024)S(1)}, s32[1024]{0:T(1024)}, u32[]{:S(2)}) copy-start(s32[1024]{0:T(1024)} %segment_ref.1) | copy-start | bytes 12292
  0.6 18.1 %copy-start.1 = (s32[128]{0:T(128)S(1)}, s32[128]{0:T(128)}, u32[]{:S(2)}) copy-start(s32[128]{0:T(128)} %param.14) | copy-start | bytes 1540
  0.7 7.8 %collective-permute-start.6 = (s32[1,128]{1,0:T(1,128)}, s32[1,128]{1,0:T(1,128)S(1)}, u32[]{:S(2)}, u32[]{:S(2)}) collective-permute-start(s32[1,128]{1,0:T(1,128)} %bitcast.16), channel_id=1, source_target_pairs={{0,7},{1,6},{2,5},{3,4},{4,3},{5,2},{6,1},{7,0},{8,15},{9,14},{10,... | collective-permute-start | bytes 1544 | tf_op jit(solution)/shard_map/ppermute | solution.py:488
  4.9 6.7 %collective-permute-start.5 = (s32[1,128]{1,0:T(1,128)}, s32[1,128]{1,0:T(1,128)S(1)}, u32[]{:S(2)}, u32[]{:S(2)}) collective-permute-start(s32[1,128]{1,0:T(1,128)} %bitcast.17), channel_id=1, source_target_pairs={{0,6},{1,7},{2,4},{3,5},{4,2},{5,3},{6,0},{7,1},{8,14},{9,15},{10,... | collective-permute-start | bytes 1544 | tf_op jit(solution)/shard_map/ppermute | solution.py:488
  6.5 8.0 %collective-permute-start.4 = (s32[1,128]{1,0:T(1,128)}, s32[1,128]{1,0:T(1,128)S(1)}, u32[]{:S(2)}, u32[]{:S(2)}) collective-permute-start(s32[1,128]{1,0:T(1,128)} %bitcast.18), channel_id=1, source_target_pairs={{0,5},{1,4},{2,7},{3,6},{4,1},{5,0},{6,3},{7,2},{8,13},{9,12},{10,... | collective-permute-start | bytes 1544 | tf_op jit(solution)/shard_map/ppermute | solution.py:488
  6.5 8.0 %collective-permute-start.3 = (s32[1,128]{1,0:T(1,128)}, s32[1,128]{1,0:T(1,128)S(1)}, u32[]{:S(2)}, u32[]{:S(2)}) collective-permute-start(s32[1,128]{1,0:T(1,128)} %bitcast.19), channel_id=1, source_target_pairs={{0,4},{1,5},{2,6},{3,7},{4,0},{5,1},{6,2},{7,3},{8,12},{9,13},{10,... | collective-permute-start | bytes 1544 | tf_op jit(solution)/shard_map/ppermute | solution.py:488
  8.2 6.4 %collective-permute-start.2 = (s32[1,128]{1,0:T(1,128)}, s32[1,128]{1,0:T(1,128)S(1)}, u32[]{:S(2)}, u32[]{:S(2)}) collective-permute-start(s32[1,128]{1,0:T(1,128)} %bitcast.20), channel_id=1, source_target_pairs={{0,3},{1,2},{2,1},{3,0},{4,7},{5,6},{6,5},{7,4},{8,11},{9,10},{10,... | collective-permute-start | bytes 1544 | tf_op jit(solution)/shard_map/ppermute | solution.py:488
  8.5 6.1 %collective-permute-start.1 = (s32[1,128]{1,0:T(1,128)}, s32[1,128]{1,0:T(1,128)S(1)}, u32[]{:S(2)}, u32[]{:S(2)}) collective-permute-start(s32[1,128]{1,0:T(1,128)} %bitcast.21), channel_id=1, source_target_pairs={{0,2},{1,3},{2,0},{3,1},{4,6},{5,7},{6,4},{7,5},{8,10},{9,11},{10,... | collective-permute-start | bytes 1544 | tf_op jit(solution)/shard_map/ppermute | solution.py:488
  11.5 3.1 %collective-permute-start = (s32[1,128]{1,0:T(1,128)}, s32[1,128]{1,0:T(1,128)S(1)}, u32[]{:S(2)}, u32[]{:S(2)}) collective-permute-start(s32[1,128]{1,0:T(1,128)} %bitcast.22), channel_id=1, source_target_pairs={{0,1},{1,0},{2,3},{3,2},{4,5},{5,4},{6,7},{7,6},{8,9},{9,8},{10,11... | collective-permute-start | bytes 1544 | tf_op jit(solution)/shard_map/ppermute | solution.py:488
  14.6 31.6 %all-to-all-start.1 = ((bf16[8,136,768]{2,1,0:T(8,128)(2,1)}), bf16[8,136,768]{2,1,0:T(8,128)(2,1)S(1)}, u32[]{:S(2)}, u32[]{:S(2)}) async-start(bf16[8,136,768]{2,1,0:T(8,128)(2,1)} %pack.1), calls=%async_computation.1 | async-start | bytes 3342336 | tf_op jit(solution)/shard_map/all_to_all | solution.py:501
  20.9 3.9 %collective-permute-start.7 = (s32[8,128]{1,0:T(8,128)S(1)}, s32[8,128]{1,0:T(8,128)S(1)}, u32[]{:S(2)}, u32[]{:S(2)}) collective-permute-start(s32[8,128]{1,0:T(8,128)S(1)} %get-tuple-element.70), channel_id=1, source_target_pairs={{0,8},{8,0},{16,24},{24,16},{32,40},{40,32},{48,56},{56,48},{64,72... | collective-permute-start | bytes 12296 | tf_op jit(solution)/shard_map/ppermute | solution.py:492
  21.3 4.3 %collective-permute-start.8 = (s32[8,128]{1,0:T(8,128)S(1)}, s32[8,128]{1,0:T(8,128)S(1)}, u32[]{:S(2)}, u32[]{:S(2)}) collective-permute-start(s32[8,128]{1,0:T(8,128)S(1)} %get-tuple-element.71), channel_id=1, source_target_pairs={{0,16},{8,24},{16,0},{24,8},{32,48},{40,56},{48,32},{56,40},{64,80... | collective-permute-start | bytes 12296 | tf_op jit(solution)/shard_map/ppermute | solution.py:492
  23.7 3.7 %collective-permute-start.9 = (s32[8,128]{1,0:T(8,128)S(1)}, s32[8,128]{1,0:T(8,128)S(1)}, u32[]{:S(2)}, u32[]{:S(2)}) collective-permute-start(s32[8,128]{1,0:T(8,128)S(1)} %get-tuple-element.72), channel_id=1, source_target_pairs={{0,24},{8,16},{16,8},{24,0},{32,56},{40,48},{48,40},{56,32},{64,88... | collective-permute-start | bytes 12296 | tf_op jit(solution)/shard_map/ppermute | solution.py:492
  28.0 10.6 %collective-permute-start.10 = (s32[4,128]{1,0:T(4,128)S(1)}, s32[4,128]{1,0:T(4,128)S(1)}, u32[]{:S(2)}, u32[]{:S(2)}) collective-permute-start(s32[4,128]{1,0:T(4,128)S(1)} %get-tuple-element.74), channel_id=1, source_target_pairs={{0,32},{8,40},{16,48},{24,56},{32,0},{40,8},{48,16},{56,24},{64,96... | collective-permute-start | bytes 6152 | tf_op jit(solution)/shard_map/ppermute | solution.py:492
  29.7 12.9 %collective-permute-start.11 = (s32[4,128]{1,0:T(4,128)S(1)}, s32[4,128]{1,0:T(4,128)S(1)}, u32[]{:S(2)}, u32[]{:S(2)}) collective-permute-start(s32[4,128]{1,0:T(4,128)S(1)} %get-tuple-element.75), channel_id=1, source_target_pairs={{0,64},{8,72},{16,80},{24,88},{32,96},{40,104},{48,112},{56,120},{... | collective-permute-start | bytes 6152 | tf_op jit(solution)/shard_map/ppermute | solution.py:492
  32.7 10.5 %collective-permute-start.12 = (s32[4,128]{1,0:T(4,128)S(1)}, s32[4,128]{1,0:T(4,128)S(1)}, u32[]{:S(2)}, u32[]{:S(2)}) collective-permute-start(s32[4,128]{1,0:T(4,128)S(1)} %get-tuple-element.76), channel_id=1, source_target_pairs={{0,96},{8,104},{16,112},{24,120},{32,64},{40,72},{48,80},{56,88},{... | collective-permute-start | bytes 6152 | tf_op jit(solution)/shard_map/ppermute | solution.py:492
  32.7 10.5 %collective-permute-start.13 = (s32[4,128]{1,0:T(4,128)S(1)}, s32[4,128]{1,0:T(4,128)S(1)}, u32[]{:S(2)}, u32[]{:S(2)}) collective-permute-start(s32[4,128]{1,0:T(4,128)S(1)} %get-tuple-element.77), channel_id=1, source_target_pairs={{0,128},{8,136},{16,144},{24,152},{32,160},{40,168},{48,176},{56,1... | collective-permute-start | bytes 6152 | tf_op jit(solution)/shard_map/ppermute | solution.py:492
  38.5 5.4 %collective-permute-start.14 = (s32[4,128]{1,0:T(4,128)S(1)}, s32[4,128]{1,0:T(4,128)S(1)}, u32[]{:S(2)}, u32[]{:S(2)}) collective-permute-start(s32[4,128]{1,0:T(4,128)S(1)} %get-tuple-element.78), channel_id=1, source_target_pairs={{0,160},{8,168},{16,176},{24,184},{32,128},{40,136},{48,144},{56,1... | collective-permute-start | bytes 6152 | tf_op jit(solution)/shard_map/ppermute | solution.py:492
  38.5 5.4 %collective-permute-start.15 = (s32[4,128]{1,0:T(4,128)S(1)}, s32[4,128]{1,0:T(4,128)S(1)}, u32[]{:S(2)}, u32[]{:S(2)}) collective-permute-start(s32[4,128]{1,0:T(4,128)S(1)} %get-tuple-element.79), channel_id=1, source_target_pairs={{0,192},{8,200},{16,208},{24,216},{32,224},{40,232},{48,240},{56,2... | collective-permute-start | bytes 6152 | tf_op jit(solution)/shard_map/ppermute | solution.py:492
  42.6 3.6 %collective-permute-start.16 = (s32[4,128]{1,0:T(4,128)S(1)}, s32[4,128]{1,0:T(4,128)S(1)}, u32[]{:S(2)}, u32[]{:S(2)}) collective-permute-start(s32[4,128]{1,0:T(4,128)S(1)} %get-tuple-element.80), channel_id=1, source_target_pairs={{0,224},{8,232},{16,240},{24,248},{32,192},{40,200},{48,208},{56,2... | collective-permute-start | bytes 6152 | tf_op jit(solution)/shard_map/ppermute | solution.py:492

commit v4 on v2

--- a/solution.py
+++ b/solution.py
@@ -9,8 +9,6 @@
 
 HEAD_DIM = 128
 N_DP = 32
-N_Z = 8
-N_X = 4
 N_SEQ = 8
 ROWS = 128
 GROUP = N_SEQ * ROWS
@@ -457,16 +455,6 @@
     return lax.all_to_all(array, "dp", split_axis=0, concat_axis=0, tiled=True)
 
 
-def relay_requests(request):
-    along_x = [[z * N_X + x for x in range(N_X)] for z in range(N_Z)]
-    along_z = [[z * N_X + x for z in range(N_Z)] for x in range(N_X)]
-    request = request.reshape(N_Z, N_X, LANES).transpose(1, 0, 2)
-    request = lax.all_to_all(request, "dp", 0, 0, axis_index_groups=along_x, tiled=True)
-    request = request.transpose(1, 0, 2)
-    request = lax.all_to_all(request, "dp", 0, 0, axis_index_groups=along_z, tiled=True)
-    return request.reshape(N_DP, LANES)
-
-
 def local(query, key_rows, value_rows, attn_out, out_grad, source_row, segment_ids):
     me = lax.axis_index("seq").reshape(1)
 
@@ -478,7 +466,9 @@
     packed, lists = lax.optimization_barrier((packed, lists))
     parts = [swap(packed[m], m) for m in range(N_SEQ)]
     rows, cols, request, most = index(me, segment_ids, lists)
-    request = relay_requests(request)
+    request, rows, cols, most, segment_ids = lax.optimization_barrier(
+        (relay(request), rows, cols, most, segment_ids)
+    )
     arrived = relay(send(me, most, request, parts))
     extra = lax.cond(
         most[0, 0] >= CAPACITY,

time: 155 us -> 153 us (0.987)
  blocking collectives: 94.8 us -> 88.3 us
  starting transfers between devices: 28 us -> 30.9 us
  waiting for transfers between devices: 6.88 us -> 9.5 us
    all_to_all x1 -> x0, blocking collectives: 8.32 us -> none  [relay_requests(): lax.all_to_all(request, 'dp', 0, 0, axis_index_groups=along_x, tiled=True)]
    all_to_all x1, starting transfers between devices: 8.19 us -> 11 us  [relay(): return lax.all_to_all(array, 'dp', split_axis=0, concat_axis=0, tiled=True)]
    all_to_all x1, waiting for transfers between devices: 5.97 us -> 8.59 us  [relay(): return lax.all_to_all(array, 'dp', split_axis=0, concat_axis=0, tiled=True)]
    all_to_all x1, blocking collectives: 65.9 us -> 68.1 us  [relay(): return lax.all_to_all(array, 'dp', split_axis=0, concat_axis=0, tiled=True)]
where the time goes in v4:
time: 153 us
  blocking collectives  88.3 us (58%)
  starting transfers between devices  30.9 us (20%)
  Pallas kernels  21.6 us (14%)
  waiting for transfers between devices  9.5 us (6%)
    all_to_all x1, blocking collectives, relay(): return lax.all_to_all(array, 'dp', split_axis=0, concat_axis=0, tiled=True)  68.1 us
    all_to_all x1, blocking collectives, local(): lax.all_to_all(grads.reshape(N_SEQ, ROWS, 4 * HEAD_DIM), 'seq', split_axi...  20.2 us
    ppermute x14, starting transfers between devices, swap(): lax.ppermute(array, 'seq', [(s, s ^ m) for s in range(N_SEQ)])  19.8 us
    all_to_all x1, starting transfers between devices, relay(): return lax.all_to_all(array, 'dp', split_axis=0, concat_axis=0, tiled=True)  11 us
    pallas_call x1, Pallas kernels, attend(): pl.pallas_call(attend_kernel, out_shape=shape((GROUP, 4 * HEAD_DIM)), in_...  10.5 us
    all_to_all x1, waiting for transfers between devices, relay(): return lax.all_to_all(array, 'dp', split_axis=0, concat_axis=0, tiled=True)  8.59 us
    pallas_call x1, Pallas kernels, send(): pl.pallas_call(send_kernel, out_shape=shape((N_DP * CAPACITY, WIDTH)), in...  5.18 us
  transfers between devices with their start and end apart: 15, of which 2 were waited for; matrix products, arithmetic and copies ran while one was open for 0% of the time, Pallas kernels for 3%

profile of v4, /device:TPU:1, one launch (start us, length us, event | category | flops | bytes accessed | tf_op | source)
XLA Modules:
  0.0 153.3 jit_solution(11485198819509576042)
XLA Ops:
  0.6 4.2 %collective-permute-start.6 = (s32[1,128]{1,0:T(1,128)}, s32[1,128]{1,0:T(1,128)S(1)}, u32[]{:S(2)}, u32[]{:S(2)}) collective-permute-start(s32[1,128]{1,0:T(1,128)} %bitcast.18), channel_id=1, source_target_pairs={{0,7},{1,6},{2,5},{3,4},{4,3},{5,2},{6,1},{7,0},{8,15},{9,14},{10,... | collective-permute-start | bytes 1544 | tf_op jit(solution)/shard_map/ppermute | solution.py:462
  4.8 1.7 %collective-permute-start.5 = (s32[1,128]{1,0:T(1,128)}, s32[1,128]{1,0:T(1,128)S(1)}, u32[]{:S(2)}, u32[]{:S(2)}) collective-permute-start(s32[1,128]{1,0:T(1,128)} %bitcast.19), channel_id=1, source_target_pairs={{0,6},{1,7},{2,4},{3,5},{4,2},{5,3},{6,0},{7,1},{8,14},{9,15},{10,... | collective-permute-start | bytes 1544 | tf_op jit(solution)/shard_map/ppermute | solution.py:462
  6.5 0.0 collective-permute-start.4
  6.5 1.7 %collective-permute-start.3 = (s32[1,128]{1,0:T(1,128)}, s32[1,128]{1,0:T(1,128)S(1)}, u32[]{:S(2)}, u32[]{:S(2)}) collective-permute-start(s32[1,128]{1,0:T(1,128)} %bitcast.21), channel_id=1, source_target_pairs={{0,4},{1,5},{2,6},{3,7},{4,0},{5,1},{6,2},{7,3},{8,12},{9,13},{10,... | collective-permute-start | bytes 1544 | tf_op jit(solution)/shard_map/ppermute | solution.py:462
  8.2 0.3 collective-permute-start.2
  8.4 0.0 collective-permute-done.6.refs_7_
  8.5 3.1 %collective-permute-start.1 = (s32[1,128]{1,0:T(1,128)}, s32[1,128]{1,0:T(1,128)S(1)}, u32[]{:S(2)}, u32[]{:S(2)}) collective-permute-start(s32[1,128]{1,0:T(1,128)} %bitcast.23), channel_id=1, source_target_pairs={{0,2},{1,3},{2,0},{3,1},{4,6},{5,7},{6,4},{7,5},{8,10},{9,11},{10,... | collective-permute-start | bytes 1544 | tf_op jit(solution)/shard_map/ppermute | solution.py:462
  11.5 0.0 collective-permute-done.5.refs_6_
  11.5 0.0 collective-permute-start
  11.5 3.0 %pack.1 = (bf16[136,768]{1,0:T(8,128)(2,1)S(1)}, bf16[136,768]{1,0:T(8,128)(2,1)}, bf16[136,768]{1,0:T(8,128)(2,1)}, bf16[136,768]{1,0:T(8,128)(2,1)}, bf16[136,...) custom-call(s32[1]{0:T(128)} %bitcast.2.me_ref, ...), custom_call_target="tpu_custom_call" | custom-call | tf_op jit(solution)/shard_map/pack/pallas_call | solution.py:361
  14.5 0.0 collective-permute-done.4.refs_5_
  14.5 0.0 collective-permute-done.3.refs_4_
  14.5 0.0 collective-permute-done.2.refs_3_
  14.5 0.0 collective-permute-done.1.refs_2_
  14.6 0.0 collective-permute-done.refs_1_
  14.6 0.6 collective-permute-start.7
  15.2 0.1 collective-permute-start.8
  15.3 1.6 %collective-permute-start.9 = (bf16[136,768]{1,0:T(8,128)(2,1)}, bf16[136,768]{1,0:T(8,128)(2,1)S(1)}, u32[]{:S(2)}, u32[]{:S(2)}) collective-permute-start(bf16[136,768]{1,0:T(8,128)(2,1)} %get-tuple-element.95), channel_id=1, source_target_pairs={{0,3},{1,2},{2,1},{3,0},{4,7},{5,6},{6,5},{7,4},{8,11},{9,10},{10,... | collective-permute-start | bytes 626696 | tf_op jit(solution)/shard_map/ppermute | solution.py:462
  16.9 1.1 collective-permute-start.10
  18.0 2.2 %collective-permute-start.11 = (bf16[136,768]{1,0:T(8,128)(2,1)}, bf16[136,768]{1,0:T(8,128)(2,1)S(1)}, u32[]{:S(2)}, u32[]{:S(2)}) collective-permute-start(bf16[136,768]{1,0:T(8,128)(2,1)} %get-tuple-element.97), channel_id=1, source_target_pairs={{0,5},{1,4},{2,7},{3,6},{4,1},{5,0},{6,3},{7,2},{8,13},{9,12},{10,... | collective-permute-start | bytes 626696 | tf_op jit(solution)/shard_map/ppermute | solution.py:462
  20.2 0.0 collective-permute-done.7.refs_1_
  20.2 1.0 collective-permute-start.12
  21.2 0.9 collective-permute-done.8.refs_2_
  22.1 2.3 %collective-permute-start.13 = (bf16[136,768]{1,0:T(8,128)(2,1)}, bf16[136,768]{1,0:T(8,128)(2,1)S(1)}, u32[]{:S(2)}, u32[]{:S(2)}) collective-permute-start(bf16[136,768]{1,0:T(8,128)(2,1)} %get-tuple-element.99), channel_id=1, source_target_pairs={{0,7},{1,6},{2,5},{3,4},{4,3},{5,2},{6,1},{7,0},{8,15},{9,14},{10,... | collective-permute-start | bytes 626696 | tf_op jit(solution)/shard_map/ppermute | solution.py:462
  24.4 0.0 copy-start
  24.4 0.7 copy-done
  25.0 0.0 copy-start.2
  25.0 0.7 copy-done.2
  25.7 1.8 %index.1 = (f32[24,128]{1,0:T(8,128)S(1)}, f32[1024,128]{1,0:T(8,128)S(1)}, s32[32,128]{1,0:T(8,128)}, s32[1,1]{1,0:T(1,128)}) custom-call(s32[1]{0:T(128)} %bitcast.2.me_ref, s32[8,128]{1,0:T(8,128)S(1)} %bitcast.17, s32[1,128]{1,0:T(1,128)S(1)} %bitcast.25, s32[1,128]{1,0:T(1,128)S(1)} %collective-permute-done.refs_1_, ...), custom_call_target="tpu_custom_call" | custom-call | tf_op jit(solution)/shard_map/index/pallas_call | solution.py:381
  27.5 11.0 %all-to-all-start.1 = ((s32[32,1,128]{2,1,0:T(1,128)}), s32[32,1,128]{2,1,0:T(1,128)S(1)}, u32[]{:S(2)}, u32[]{:S(2)}) async-start(s32[32,1,128]{2,1,0:T(1,128)} %bitcast.6), calls=%async_computation.1 | async-start | bytes 32768 | tf_op jit(solution)/shard_map/all_to_all | solution.py:455
  38.6 8.6 %all-to-all-done.1 = s32[32,1,128]{2,1,0:T(1,128)S(1)} async-done(((s32[32,1,128]{2,1,0:T(1,128)}), s32[32,1,128]{2,1,0:T(1,128)S(1)}, u32[]{:S(2)}, u32[]{:S(2)}) %all-to-all-start.1) | async-done | bytes 16416 | tf_op jit(solution)/shard_map/all_to_all | solution.py:455
  47.9 0.0 collective-permute-done.9.refs_3_
  47.9 0.0 collective-permute-done.10.refs_4_
  47.9 0.0 collective-permute-done.11.refs_5_
  47.9 0.0 collective-permute-done.12.refs_6_
  47.9 0.0 collective-permute-done.13.refs_7_
  47.9 0.3 conditional.1
  47.9 0.1 broadcast.2
  48.2 5.2 %send.1 = bf16[1792,768]{1,0:T(8,128)(2,1)S(1)} custom-call(s32[1]{0:T(128)} %bitcast.2.me_ref, s32[1,1]{1,0:T(1,128)} %get-tuple-element.90.most_ref, s32[32,128]{1,0:T(8,128)S(1)} %bitcast.28, bf16[136,768]{1,0:T(8,128)(2,1)S(1)} %get-tuple-element.92.refs_0_, bf16[136,768]{1,0:T(8,128)(2,1)S(1)} %collective-permute-done.7.refs_1_, ...), custom_call_target="tpu_custom_call" | custom-call | flops 2818572288 | bytes 4000000 | tf_op jit(solution)/shard_map/send/pallas_call | solution.py:398
  53.4 0.0 copy-start.1
  53.4 68.1 %all_to_all.38 = bf16[32,56,768]{2,1,0:T(8,128)(2,1)S(1)} all-to-all(bf16[32,56,768]{2,1,0:T(8,128)(2,1)S(1)} %bitcast.16), channel_id=1, replica_groups=mesh['dp'=32,'seq'=8] {'dp'}, dimensions={0} | all-to-all | bytes 5505024 | tf_op jit(solution)/shard_map/all_to_all | solution.py:455
  121.5 0.0 copy-done.1
  121.5 10.5 %attend.1 = bf16[1024,512]{1,0:T(8,128)(2,1)S(1)} custom-call(s32[1024]{0:T(1024)S(1)} %copy-done.1, s32[1,1]{1,0:T(1,128)} %get-tuple-element.90.most_ref, bf16[1792,768]{1,0:T(8,128)(2,1)S(1)} %bitcast.13, bf16[512,768]{1,0:T(8,128)(2,1)S(1)} %get-tuple-element.102.extra_ref, f32[24,128]{1,0:T(8,128)S(1)} %get-tuple-element.100.rows_ref, ...), custom_call_target="tpu_custom_call" | custom-call | tf_op jit(solution)/shard_map/attend/pallas_call | solution.py:425
  132.0 20.2 %all_to_all.39.returned_ref = bf16[8,128,512]{2,1,0:T(8,128)(2,1)S(1)} all-to-all(bf16[8,128,512]{2,1,0:T(8,128)(2,1)S(1)} %bitcast.14), channel_id=1, replica_groups=mesh['dp'=32,'seq'=8] {'seq'}, dimensions={0} | all-to-all | bytes 2097152 | tf_op jit(solution)/shard_map/all_to_all | solution.py:481
  152.1 1.2 unpack.1
Async XLA Ops:
  0.6 7.8 %collective-permute-start.6 = (s32[1,128]{1,0:T(1,128)}, s32[1,128]{1,0:T(1,128)S(1)}, u32[]{:S(2)}, u32[]{:S(2)}) collective-permute-start(s32[1,128]{1,0:T(1,128)} %bitcast.18), channel_id=1, source_target_pairs={{0,7},{1,6},{2,5},{3,4},{4,3},{5,2},{6,1},{7,0},{8,15},{9,14},{10,... | collective-permute-start | bytes 1544 | tf_op jit(solution)/shard_map/ppermute | solution.py:462
  4.8 6.7 %collective-permute-start.5 = (s32[1,128]{1,0:T(1,128)}, s32[1,128]{1,0:T(1,128)S(1)}, u32[]{:S(2)}, u32[]{:S(2)}) collective-permute-start(s32[1,128]{1,0:T(1,128)} %bitcast.19), channel_id=1, source_target_pairs={{0,6},{1,7},{2,4},{3,5},{4,2},{5,3},{6,0},{7,1},{8,14},{9,15},{10,... | collective-permute-start | bytes 1544 | tf_op jit(solution)/shard_map/ppermute | solution.py:462
  6.5 8.0 %collective-permute-start.4 = (s32[1,128]{1,0:T(1,128)}, s32[1,128]{1,0:T(1,128)S(1)}, u32[]{:S(2)}, u32[]{:S(2)}) collective-permute-start(s32[1,128]{1,0:T(1,128)} %bitcast.20), channel_id=1, source_target_pairs={{0,5},{1,4},{2,7},{3,6},{4,1},{5,0},{6,3},{7,2},{8,13},{9,12},{10,... | collective-permute-start | bytes 1544 | tf_op jit(solution)/shard_map/ppermute | solution.py:462
  6.5 8.0 %collective-permute-start.3 = (s32[1,128]{1,0:T(1,128)}, s32[1,128]{1,0:T(1,128)S(1)}, u32[]{:S(2)}, u32[]{:S(2)}) collective-permute-start(s32[1,128]{1,0:T(1,128)} %bitcast.21), channel_id=1, source_target_pairs={{0,4},{1,5},{2,6},{3,7},{4,0},{5,1},{6,2},{7,3},{8,12},{9,13},{10,... | collective-permute-start | bytes 1544 | tf_op jit(solution)/shard_map/ppermute | solution.py:462
  8.2 6.3 %collective-permute-start.2 = (s32[1,128]{1,0:T(1,128)}, s32[1,128]{1,0:T(1,128)S(1)}, u32[]{:S(2)}, u32[]{:S(2)}) collective-permute-start(s32[1,128]{1,0:T(1,128)} %bitcast.22), channel_id=1, source_target_pairs={{0,3},{1,2},{2,1},{3,0},{4,7},{5,6},{6,5},{7,4},{8,11},{9,10},{10,... | collective-permute-start | bytes 1544 | tf_op jit(solution)/shard_map/ppermute | solution.py:462
  8.5 6.1 %collective-permute-start.1 = (s32[1,128]{1,0:T(1,128)}, s32[1,128]{1,0:T(1,128)S(1)}, u32[]{:S(2)}, u32[]{:S(2)}) collective-permute-start(s32[1,128]{1,0:T(1,128)} %bitcast.23), channel_id=1, source_target_pairs={{0,2},{1,3},{2,0},{3,1},{4,6},{5,7},{6,4},{7,5},{8,10},{9,11},{10,... | collective-permute-start | bytes 1544 | tf_op jit(solution)/shard_map/ppermute | solution.py:462
  11.5 3.0 %collective-permute-start = (s32[1,128]{1,0:T(1,128)}, s32[1,128]{1,0:T(1,128)S(1)}, u32[]{:S(2)}, u32[]{:S(2)}) collective-permute-start(s32[1,128]{1,0:T(1,128)} %bitcast.24), channel_id=1, source_target_pairs={{0,1},{1,0},{2,3},{3,2},{4,5},{5,4},{6,7},{7,6},{8,9},{9,8},{10,11... | collective-permute-start | bytes 1544 | tf_op jit(solution)/shard_map/ppermute | solution.py:462
  14.6 5.6 %collective-permute-start.7 = (bf16[136,768]{1,0:T(8,128)(2,1)}, bf16[136,768]{1,0:T(8,128)(2,1)S(1)}, u32[]{:S(2)}, u32[]{:S(2)}) collective-permute-start(bf16[136,768]{1,0:T(8,128)(2,1)} %get-tuple-element.93), channel_id=1, source_target_pairs={{0,1},{1,0},{2,3},{3,2},{4,5},{5,4},{6,7},{7,6},{8,9},{9,8},{10,11... | collective-permute-start | bytes 626696 | tf_op jit(solution)/shard_map/ppermute | solution.py:462
  15.2 6.9 %collective-permute-start.8 = (bf16[136,768]{1,0:T(8,128)(2,1)}, bf16[136,768]{1,0:T(8,128)(2,1)S(1)}, u32[]{:S(2)}, u32[]{:S(2)}) collective-permute-start(bf16[136,768]{1,0:T(8,128)(2,1)} %get-tuple-element.94), channel_id=1, source_target_pairs={{0,2},{1,3},{2,0},{3,1},{4,6},{5,7},{6,4},{7,5},{8,10},{9,11},{10,... | collective-permute-start | bytes 626696 | tf_op jit(solution)/shard_map/ppermute | solution.py:462
  15.3 32.6 %collective-permute-start.9 = (bf16[136,768]{1,0:T(8,128)(2,1)}, bf16[136,768]{1,0:T(8,128)(2,1)S(1)}, u32[]{:S(2)}, u32[]{:S(2)}) collective-permute-start(bf16[136,768]{1,0:T(8,128)(2,1)} %get-tuple-element.95), channel_id=1, source_target_pairs={{0,3},{1,2},{2,1},{3,0},{4,7},{5,6},{6,5},{7,4},{8,11},{9,10},{10,... | collective-permute-start | bytes 626696 | tf_op jit(solution)/shard_map/ppermute | solution.py:462
  16.9 31.0 %collective-permute-start.10 = (bf16[136,768]{1,0:T(8,128)(2,1)}, bf16[136,768]{1,0:T(8,128)(2,1)S(1)}, u32[]{:S(2)}, u32[]{:S(2)}) collective-permute-start(bf16[136,768]{1,0:T(8,128)(2,1)} %get-tuple-element.96), channel_id=1, source_target_pairs={{0,4},{1,5},{2,6},{3,7},{4,0},{5,1},{6,2},{7,3},{8,12},{9,13},{10,... | collective-permute-start | bytes 626696 | tf_op jit(solution)/shard_map/ppermute | solution.py:462
  18.0 29.9 %collective-permute-start.11 = (bf16[136,768]{1,0:T(8,128)(2,1)}, bf16[136,768]{1,0:T(8,128)(2,1)S(1)}, u32[]{:S(2)}, u32[]{:S(2)}) collective-permute-start(bf16[136,768]{1,0:T(8,128)(2,1)} %get-tuple-element.97), channel_id=1, source_target_pairs={{0,5},{1,4},{2,7},{3,6},{4,1},{5,0},{6,3},{7,2},{8,13},{9,12},{10,... | collective-permute-start | bytes 626696 | tf_op jit(solution)/shard_map/ppermute | solution.py:462
  20.2 27.7 %collective-permute-start.12 = (bf16[136,768]{1,0:T(8,128)(2,1)}, bf16[136,768]{1,0:T(8,128)(2,1)S(1)}, u32[]{:S(2)}, u32[]{:S(2)}) collective-permute-start(bf16[136,768]{1,0:T(8,128)(2,1)} %get-tuple-element.98), channel_id=1, source_target_pairs={{0,6},{1,7},{2,4},{3,5},{4,2},{5,3},{6,0},{7,1},{8,14},{9,15},{10,... | collective-permute-start | bytes 626696 | tf_op jit(solution)/shard_map/ppermute | solution.py:462
  22.1 25.8 %collective-permute-start.13 = (bf16[136,768]{1,0:T(8,128)(2,1)}, bf16[136,768]{1,0:T(8,128)(2,1)S(1)}, u32[]{:S(2)}, u32[]{:S(2)}) collective-permute-start(bf16[136,768]{1,0:T(8,128)(2,1)} %get-tuple-element.99), channel_id=1, source_target_pairs={{0,7},{1,6},{2,5},{3,4},{4,3},{5,2},{6,1},{7,0},{8,15},{9,14},{10,... | collective-permute-start | bytes 626696 | tf_op jit(solution)/shard_map/ppermute | solution.py:462
  24.4 0.7 copy-start
  25.0 0.7 copy-start.2
  27.5 19.7 %all-to-all-start.1 = ((s32[32,1,128]{2,1,0:T(1,128)}), s32[32,1,128]{2,1,0:T(1,128)S(1)}, u32[]{:S(2)}, u32[]{:S(2)}) async-start(s32[32,1,128]{2,1,0:T(1,128)} %bitcast.6), calls=%async_computation.1 | async-start | bytes 32768 | tf_op jit(solution)/shard_map/all_to_all | solution.py:455
  53.4 68.1 %copy-start.1 = (s32[1024]{0:T(1024)S(1)}, s32[1024]{0:T(1024)}, u32[]{:S(2)}) copy-start(s32[1024]{0:T(1024)} %segment_ref) | copy-start | bytes 12292
